TPU v7x, 256 devices: a whole 4x4x8 slice. The times are simulated.
256 devices in a mesh: ctx: 32 (over y_hi, z, core), tp: 8 (over x, y_lo).
Axes of the slice: x: 4, y: 4 (y_hi: 2, y_lo: 2; y = y_hi * 2 + y_lo), z: 8, core: 2. Of those that a mesh axis runs over, the one named last changes fastest.
Arguments:
- qkv: bfloat16 [3, 4096, 4096], P(None, 'tp', 'ctx'), may hold values from -6 to 6
- short_w: float32 [3, 3, 4096], P(None, None, ('tp', 'ctx')), may hold values from -1 to 1
- filters: float32 [4096, 4096], P(('tp', 'ctx')), may hold values from -0.09375 to 0.09375
- skip: float32 [4096], P(('tp', 'ctx')), may hold values from -4 to 4
- w_out: bfloat16 [4096, 4096], P('tp', 'ctx'), may hold values from -0.09375 to 0.09375
- grad_out: bfloat16 [4096, 4096], P('ctx', 'tp'), may hold values from -6 to 6
Outputs:
- output: bfloat16 [4096, 4096], P('ctx', 'tp')
- grad_qkv: bfloat16 [3, 4096, 4096], P(None, 'tp', 'ctx')
- grad_filters: float32 [4096, 4096], P(('tp', 'ctx'))
- grad_w_out: float32 [4096, 4096], P('tp', 'ctx')
All inputs are finite; a program needn't handle non-finite values.
Results may differ from a plain program's by a relative error of at most 0.02.
Values may be sent and summed in bfloat16 or wider, within the bound.
No kernel may reach another device: no remote copies, remote signals or barrier semaphores. Data moves between devices by JAX's collectives and lax.ppermute only.
A program may use at most 64 MiB of HBM per device.

v0:
```python
import functools
import math

import jax
import jax.numpy as jnp
import ml_dtypes
import numpy as np
from jax import lax
from jax.experimental import pallas as pl
from jax.experimental.pallas import tpu as pltpu
from jax.sharding import PartitionSpec as P

F32 = jnp.float32
BF16 = jnp.bfloat16
SEQ = 4096
CH = 16
SH = 32
LN = 128
HALF = 40
VM = pl.BlockSpec(memory_space=pltpu.VMEM)
SM = pl.BlockSpec(memory_space=pltpu.SMEM)
PARAMS = pltpu.CompilerParams(vmem_limit_bytes=48 * 1024 * 1024)


def split(table):
    high = table.astype(ml_dtypes.bfloat16)
    low = (table - high.astype(np.float64)).astype(ml_dtypes.bfloat16)
    return np.stack([high, low])


def tables():
    d = np.arange(HALF)[:, None]
    live = d <= 32
    a = np.arange(SH)[None, :]
    b = np.arange(LN)
    one = 2 * math.pi * d * a / 64
    first = np.concatenate([np.cos(one) * live, -np.sin(one) * live], axis=0)
    turn = 2 * math.pi * d * b[None, :] / 8192
    twist = np.stack([np.cos(turn), np.sin(turn)]).astype(np.float32)
    two = 2 * math.pi * b[:, None] * b[None, :] / 128
    c2, s2 = np.cos(two), np.sin(two)
    second = np.block([[c2, -s2], [s2, c2]])
    back = np.block([[c2, s2], [-s2, c2]])
    weight = np.where((d == 0) | (d == 32), 1.0, 2.0) * live / 8192
    last = np.concatenate([(np.cos(one) * weight).T, (-np.sin(one) * weight).T], axis=1)
    return split(first), twist, split(second), split(back), split(last)


def parts(values):
    high = values.astype(BF16)
    low = (values - high.astype(F32)).astype(BF16)
    return high, low


def dot(left, right):
    return lax.dot_general(left, right, (((1,), (0,)), ((), ())), preferred_element_type=F32)


def table_left(table, values):
    high, low = parts(values)
    return dot(table[0], high) + dot(table[0], low) + dot(table[1], high)


def table_right(values, table):
    high, low = parts(values)
    return dot(high, table[0]) + dot(low, table[0]) + dot(high, table[1])


def column(c):
    return slice(c * LN, (c + 1) * LN)


def forward(values, first, twist, second, work):
    grid = table_left(first, values)
    cosine, sine = twist[0], twist[1]
    for c in range(CH):
        real, imag = grid[:HALF, column(c)], grid[HALF:, column(c)]
        work[c * HALF : (c + 1) * HALF, :LN] = real * cosine + imag * sine
        work[c * HALF : (c + 1) * HALF, LN:] = imag * cosine - real * sine
    return table_right(work[...], second)


def inverse(spectrum, twist, back, last):
    grid = table_right(spectrum, back)
    cosine, sine = twist[0], twist[1]
    columns = []
    for c in range(CH):
        real = grid[c * HALF : (c + 1) * HALF, :LN]
        imag = grid[c * HALF : (c + 1) * HALF, LN:]
        columns.append(
            jnp.concatenate([real * cosine - imag * sine, imag * cosine + real * sine], axis=0)
        )
    return table_left(last, jnp.concatenate(columns, axis=1))


def times(first, second, conjugate):
    ar, ai = first[:, :LN], first[:, LN:]
    br, bi = second[:, :LN], second[:, LN:]
    if conjugate:
        return jnp.concatenate([ar * br + ai * bi, ar * bi - ai * br], axis=1)
    return jnp.concatenate([ar * br - ai * bi, ar * bi + ai * br], axis=1)


def lane_row():
    lane = lax.broadcasted_iota(jnp.int32, (SH, LN), 1)
    row = lax.broadcasted_iota(jnp.int32, (SH, LN), 0)
    return lane, row


def later(values, steps, lane, row):
    here = pltpu.roll(values, steps, 1)
    above = jnp.where(row >= 1, pltpu.roll(here, 1, 0), 0.0)
    return jnp.where(lane >= steps, here, above)


def sooner(values, steps, lane, row):
    here = pltpu.roll(values, LN - steps, 1)
    below = jnp.where(row < SH - 1, pltpu.roll(here, SH - 1, 0), 0.0)
    return jnp.where(lane < LN - steps, here, below)


def filter_kernel(filters, first, twist, second, spectrum, rows, work):
    for a in range(SH):
        rows[pl.ds(a, CH, stride=SH), :] = filters[:, column(a)]
    values = jnp.concatenate([rows[c * SH : (c + 1) * SH, :] for c in range(CH)], axis=1)
    spectrum[...] = forward(values, first, twist, second, work)


def front_kernel(
    streams, short_w, skip, kernel, first, twist, second, back, last,
    outgoing, query, left, right, signal, spectrum, rows, work, packed,
):
    lane, row = lane_row()
    for j in range(SH):
        rows[j * 48 : (j + 1) * 48, :] = streams[j].astype(F32)
    gated = []
    for c in range(CH):
        conv = []
        for s in range(3):
            x = rows[pl.ds(s * CH + c, SH, stride=48), :]
            y = short_w[s, 0, c] * x
            y = y + short_w[s, 1, c] * later(x, 1, lane, row)
            y = y + short_w[s, 2, c] * later(x, 2, lane, row)
            conv.append(y)
        query[:, column(c)] = conv[0].astype(BF16).astype(F32)
        left[:, column(c)] = conv[1]
        right[:, column(c)] = conv[2]
        gated.append((conv[1] * conv[2]).astype(BF16).astype(F32))
    own = forward(jnp.concatenate(gated, axis=1), first, twist, second, work)
    spectrum[...] = own
    total = inverse(times(kernel[...], own, False), twist, back, last)
    for c in range(CH):
        value = total[:, column(c)] + skip[c] * gated[c]
        signal[:, column(c)] = value
        packed[pl.ds(c, SH, stride=CH), :] = query[:, column(c)] * value
    for high in range(2):
        for low in range(4):
            for q in range(4):
                j = high * 16 + q * 4 + low
                piece = packed[j * CH : (j + 1) * CH, :].astype(BF16)
                for target in range(4):
                    outgoing[high * 16 + target * 4 + low, :, column(q)] = piece


def rear_kernel(
    upstream, short_w, skip, kernel, spectrum, query, left, right, signal,
    first, twist, second, back, last,
    outgoing, grad_filters, rows, work, packed, turned,
):
    lane, row = lane_row()
    for high in range(2):
        for low in range(4):
            total = upstream[high * 16 + low].astype(F32)
            for q in range(1, 4):
                total = total + upstream[high * 16 + q * 4 + low].astype(F32)
            for q in range(4):
                j = high * 16 + q * 4 + low
                rows[j * CH : (j + 1) * CH, :] = total[:, column(q)]

    def emit(s, c, x):
        y = short_w[s, 0, c] * x
        y = y + short_w[s, 1, c] * sooner(x, 1, lane, row)
        y = y + short_w[s, 2, c] * sooner(x, 2, lane, row)
        packed[pl.ds(s * CH + c, SH, stride=48), :] = y

    grad_signal = []
    for c in range(CH):
        up = rows[pl.ds(c, SH, stride=CH), :]
        grad_signal.append(up * query[:, column(c)])
        emit(0, c, (up * signal[:, column(c)]).astype(BF16).astype(F32))
    own = forward(jnp.concatenate(grad_signal, axis=1), first, twist, second, work)
    through = inverse(times(kernel[...], own, True), twist, back, last)
    for c in range(CH):
        grad = (through[:, column(c)] + skip[c] * grad_signal[c]).astype(BF16).astype(F32)
        emit(1, c, grad * right[:, column(c)])
        emit(2, c, grad * left[:, column(c)])
    for j in range(SH):
        outgoing[j] = packed[j * 48 : (j + 1) * 48, :].astype(BF16)
    taps = inverse(times(spectrum[...], own, True), twist, back, last)
    for c in range(CH):
        turned[c * SH : (c + 1) * SH, :] = taps[:, column(c)] * (SEQ**-0.5)
    for a in range(SH):
        grad_filters[:, column(a)] = turned[pl.ds(a, CH, stride=SH), :]


def weight_blocks(place, near, far, weight):
    for flip, blocks in ((0, near), (1, far)):
        for k in range(4):
            high = place[0] ^ (k >> 1)
            low = (place[1] ^ (k & 1)) * 2 + (place[2] ^ flip)
            weight[high, :, pl.ds(pl.multiple_of(low * LN, LN), LN)] = blocks[k]


def token_blocks(place, near, far, grad):
    for flip, blocks in ((0, near), (1, far)):
        for k in range(4):
            high = place[3] ^ (k >> 1)
            low = (place[4] ^ (k & 1)) * 2 + (place[5] ^ flip)
            grad[high, pl.ds(pl.multiple_of(low * LN, LN), LN), :] = blocks[k]


def product(left, right, over):
    return lax.dot_general(left, right, ((over[:1], over[1:]), ((), ())), preferred_element_type=F32)


def mixed_grad_kernel(place, w_near, w_far, g_near, g_far, _, outgoing, weight, grad):
    weight_blocks(place, w_near, w_far, weight)
    token_blocks(place, g_near, g_far, grad)
    for half in range(2):
        rows = slice(half * 256, (half + 1) * 256)
        total = product(weight[0, rows, :], grad[0], (1, 1))
        total = total + product(weight[1, rows, :], grad[1], (1, 1))
        outgoing[half * 16 : (half + 1) * 16] = total.astype(BF16).reshape(16, CH, 512)


def projection_kernel(
    place, mixed, w_near, w_far, g_near, g_far, o_near, o_far, d_near, d_far, weight, grad, held
):
    weight_blocks(place, w_near, w_far, weight)
    token_blocks(place, g_near, g_far, grad)
    rows = mixed[...].reshape(512, 512)
    for high in range(2):
        held[high] = product(rows, weight[high], (0, 0)).astype(BF16)
    for flip, blocks in ((0, o_near), (1, o_far)):
        for k in range(4):
            high = place[3] ^ (k >> 1)
            low = (place[4] ^ (k & 1)) * 2 + (place[5] ^ flip)
            blocks[k] = held[high, pl.ds(pl.multiple_of(low * LN, LN), LN), :]
    for high in range(2):
        held[high] = product(rows, grad[high], (1, 0)).astype(BF16)
    for flip, blocks in ((0, d_near), (1, d_far)):
        for k in range(4):
            high = place[0] ^ (k >> 1)
            low = (place[1] ^ (k & 1)) * 2 + (place[2] ^ flip)
            blocks[k] = held[high, :, pl.ds(pl.multiple_of(low * LN, LN), LN)]


def flat(*shape):
    return jax.ShapeDtypeStruct(shape, F32)


def half(*shape):
    return jax.ShapeDtypeStruct(shape, BF16)


def flip(values, axis, size, mask):
    return lax.ppermute(values, axis, [(i, i ^ mask) for i in range(size)])


def exchange(values):
    pairs = []
    for j in range(32):
        for i in range(8):
            to_j = (j & 0b10011) | ((i & 3) << 2)
            to_i = (i & 4) | ((j >> 2) & 3)
            pairs.append((j * 8 + i, to_j * 8 + to_i))
    return lax.ppermute(values, ("ctx", "tp"), pairs)


def shards(qkv, short_w, filters, skip, w_out, grad_out):
    first, twist, second, back, last = [jnp.asarray(t) for t in tables()]
    j, i = lax.axis_index("ctx"), lax.axis_index("tp")
    place = jnp.stack([j >> 4, (j >> 1) & 1, j & 1, i >> 2, (i >> 1) & 1, i & 1]).astype(jnp.int32)

    w_near = jnp.stack([w_out] + [flip(w_out, "ctx", 32, m) for m in (2, 16, 18)])
    w_far = flip(w_near, "ctx", 32, 1)
    tile = exchange(grad_out)
    g_near = jnp.stack([tile] + [flip(tile, "tp", 8, m) for m in (2, 4, 6)])
    g_far = flip(g_near, "tp", 8, 1)

    sent = qkv.reshape(3, SH, CH, LN).transpose(1, 0, 2, 3).reshape(SH, 3 * CH, LN)
    streams = lax.all_to_all(sent, "ctx", 0, 0)

    kernel = pl.pallas_call(
        filter_kernel,
        out_shape=flat(CH * HALF, 2 * LN),
        in_specs=[VM] * 4,
        out_specs=VM,
        scratch_shapes=[pltpu.VMEM((CH * SH, LN), F32), pltpu.VMEM((CH * HALF, 2 * LN), F32)],
        compiler_params=PARAMS,
        name="filter_spectrum",
    )(filters, first, twist, second)

    buffer, query, left, right, signal, spectrum = pl.pallas_call(
        front_kernel,
        out_shape=[half(SH, 2 * CH, 512)] + [flat(SH, CH * LN)] * 4 + [flat(CH * HALF, 2 * LN)],
        in_specs=[VM, SM, SM] + [VM] * 6,
        out_specs=[pl.BlockSpec((SH, CH, 512), lambda g: (0, 0, 0))] + [VM] * 5,
        scratch_shapes=[
            pltpu.VMEM((SH * 48, LN), F32),
            pltpu.VMEM((CH * HALF, 2 * LN), F32),
            pltpu.VMEM((SH * CH, LN), F32),
        ],
        grid=(1,),
        compiler_params=PARAMS,
        name="front",
    )(streams, short_w, skip, kernel, first, twist, second, back, last)

    buffer = pl.pallas_call(
        mixed_grad_kernel,
        out_shape=half(SH, 2 * CH, 512),
        in_specs=[SM] + [VM] * 4 + [pl.BlockSpec(memory_space=pl.ANY)],
        out_specs=pl.BlockSpec((SH, CH, 512), lambda g: (0, 1, 0)),
        scratch_shapes=[pltpu.VMEM((2, 512, 512), BF16), pltpu.VMEM((2, 512, 512), BF16)],
        input_output_aliases={5: 0},
        grid=(1,),
        compiler_params=PARAMS,
        name="mixed_grad",
    )(place, w_near, w_far, g_near, g_far, buffer)

    joint = lax.all_to_all(buffer, "ctx", 0, 0)

    o_near, o_far, d_near, d_far = pl.pallas_call(
        projection_kernel,
        out_shape=[half(4, LN, 512)] * 2 + [half(4, 512, LN)] * 2,
        in_specs=[SM, pl.BlockSpec((SH, CH, 512), lambda g: (0, 0, 0))] + [VM] * 4,
        out_specs=[VM] * 4,
        scratch_shapes=[pltpu.VMEM((2, 512, 512), BF16)] * 3,
        grid=(1,),
        compiler_params=PARAMS,
        name="projections",
    )(place, joint, w_near, w_far, g_near, g_far)

    o_sum = o_near.astype(F32) + flip(o_far, "tp", 8, 1).astype(F32)
    o_sent = o_sum.astype(BF16)
    o_total = o_sum[0]
    for k in range(1, 4):
        o_total = o_total + flip(o_sent[k], "tp", 8, 2 * k).astype(F32)
    output = exchange(o_total.astype(BF16))

    d_sum = d_near.astype(F32) + flip(d_far, "ctx", 32, 1).astype(F32)
    d_sent = d_sum.astype(BF16)
    d_total = d_sum[0]
    for k, m in ((1, 2), (2, 16), (3, 18)):
        d_total = d_total + flip(d_sent[k], "ctx", 32, m).astype(F32)
    grad_w_out = d_total * (SEQ**-0.5)

    grads, grad_filters = pl.pallas_call(
        rear_kernel,
        out_shape=[half(SH, 3 * CH, LN), flat(CH, SEQ)],
        in_specs=[pl.BlockSpec((SH, CH, 512), lambda g: (0, 1, 0)), SM, SM] + [VM] * 11,
        out_specs=[VM, VM],
        scratch_shapes=[
            pltpu.VMEM((SH * CH, LN), F32),
            pltpu.VMEM((CH * HALF, 2 * LN), F32),
            pltpu.VMEM((SH * 48, LN), F32),
            pltpu.VMEM((CH * SH, LN), F32),
        ],
        grid=(1,),
        compiler_params=PARAMS,
        name="rear",
    )(joint, short_w, skip, kernel, spectrum, query, left, right, signal, first, twist, second, back, last)

    returned = lax.all_to_all(grads, "ctx", 0, 0)
    grad_qkv = returned.reshape(SH, 3, CH, LN).transpose(1, 0, 2, 3).reshape(3, SH * CH, LN)
    return (output, grad_qkv, grad_filters, grad_w_out)


def solution(mesh):
    placed = (
        P(None, "tp", "ctx"),
        P(None, None, ("tp", "ctx")),
        P(("tp", "ctx"), None),
        P(("tp", "ctx")),
        P("tp", "ctx"),
        P("ctx", "tp"),
    )
    return jax.shard_map(
        shards,
        mesh=mesh,
        in_specs=placed,
        out_specs=(P("ctx", "tp"), P(None, "tp", "ctx"), P(("tp", "ctx"), None), P("tp", "ctx")),
        check_vma=False,
    )
```

profile of v0, /device:TPU:42, one launch (start us, length us, event | category | flops | bytes accessed | tf_op | source)
XLA Modules:
  0.0 134.5 jit_solution(6728801298945839176)
XLA Ops:
  0.6 7.2 %collective-permute-start.4 = (bf16[128,512]{1,0:T(8,128)(2,1)}, bf16[128,512]{1,0:T(8,128)(2,1)S(1)}, u32[]{:S(2)}, u32[]{:S(2)}) collective-permute-start(bf16[128,512]{1,0:T(8,128)(2,1)} %param.16), channel_id=1, source_target_pairs={{0,0},{1,32},{2,64},{3,96},{4,4},{5,36},{6,68},{7,100},{8,8},{9,40... | collective-permute-start | bytes 393224 | tf_op jit(solution)/shard_map/ppermute | solution.py:277
  7.8 1.1 collective-permute-start
  8.9 3.0 %collective-permute-start.2 = (bf16[512,128]{1,0:T(8,128)(2,1)}, bf16[512,128]{1,0:T(8,128)(2,1)S(1)}, u32[]{:S(2)}, u32[]{:S(2)}) collective-permute-start(bf16[512,128]{1,0:T(8,128)(2,1)} %param.15), channel_id=1, source_target_pairs={{0,144},{8,152},{16,128},{24,136},{32,176},{40,184},{48,160},{56,1... | collective-permute-start | bytes 393224 | tf_op jit(solution)/shard_map/ppermute | solution.py:267
  11.9 0.9 collective-permute-start.1
  12.9 6.0 %collective-permute-done.4 = bf16[128,512]{1,0:T(8,128)(2,1)S(1)} collective-permute-done((bf16[128,512]{1,0:T(8,128)(2,1)}, bf16[128,512]{1,0:T(8,128)(2,1)S(1)}, u32[]{:S(2)}, u32[]{:S(2)}) %collective-permute-start.4) | collective-permute-done | bytes 131104 | tf_op jit(solution)/shard_map/ppermute | solution.py:277
  18.9 1.8 %collective-permute-start.6 = (bf16[128,512]{1,0:T(8,128)(2,1)S(1)}, bf16[128,512]{1,0:T(8,128)(2,1)S(1)}, u32[]{:S(2)}, u32[]{:S(2)}) collective-permute-start(bf16[128,512]{1,0:T(8,128)(2,1)S(1)} %collective-permute-done.4), channel_id=1, source_target_pairs={{0,4},{1,5},{2,6},{3,7},{4,0},{5,1},{6,2},{7,3},{8,12},{9,13},{10,... | collective-permute-start | bytes 393224 | tf_op jit(solution)/shard_map/ppermute | solution.py:267
  20.8 2.3 %collective-permute-start.5 = (bf16[128,512]{1,0:T(8,128)(2,1)S(1)}, bf16[128,512]{1,0:T(8,128)(2,1)S(1)}, u32[]{:S(2)}, u32[]{:S(2)}) collective-permute-start(bf16[128,512]{1,0:T(8,128)(2,1)S(1)} %collective-permute-done.4), channel_id=1, source_target_pairs={{0,2},{1,3},{2,0},{3,1},{4,6},{5,7},{6,4},{7,5},{8,10},{9,11},{10,... | collective-permute-start | bytes 393224 | tf_op jit(solution)/shard_map/ppermute | solution.py:267
  23.0 1.8 %copy.16 = bf16[3,32,16,128]{3,2,0,1:T(8,128)(2,1)} copy(bf16[3,32,16,128]{3,2,1,0:T(8,128)(2,1)} %bitcast.55) | data formatting | bytes 786432 | tf_op jit(solution)/shard_map/reshape | solution.py:291
  24.8 8.3 %all-to-all-start = ((bf16[32,48,128]{2,1,0:T(8,128)(2,1)}), bf16[32,48,128]{2,1,0:T(8,128)(2,1)S(1)}, u32[]{:S(2)}, u32[]{:S(2)}) async-start(bf16[32,48,128]{2,1,0:T(8,128)(2,1)} %bitcast.16), calls=%async_computation | async-start | bytes 786432 | tf_op jit(solution)/shard_map/all_to_all | solution.py:292
  33.1 0.1 pad_maximum_fusion.w_near
  33.2 0.2 collective-permute-start.3
  33.4 0.0 copy-start
  33.5 0.0 copy-start.5
  33.5 0.0 copy-start.7
  33.5 0.1 pad_maximum_fusion.1.g_near
  33.6 1.0 collective-permute-start.8
  34.6 0.9 copy-done.9
  35.5 0.9 filter_spectrum.1.kernel
  36.4 0.1 stack.57.place
  36.5 13.1 %all-to-all-done.streams = bf16[32,48,128]{2,1,0:T(8,128)(2,1)S(1)} async-done(((bf16[32,48,128]{2,1,0:T(8,128)(2,1)}), bf16[32,48,128]{2,1,0:T(8,128)(2,1)S(1)}, u32[]{:S(2)}, u32[]{:S(2)}) %all-to-all-start) | async-done | bytes 393248 | tf_op jit(solution)/shard_map/all_to_all | solution.py:292
  49.7 0.9 copy-done.1
  50.6 2.9 %front.1 = (bf16[32,32,512]{2,1,0:T(8,128)(2,1)S(1)}, f32[32,2048]{1,0:T(8,128)S(1)}, f32[32,2048]{1,0:T(8,128)S(1)}, f32[32,2048]{1,0:T(8,128)S(1)}, f32[32,2048]{1,0:T(8,128)S(1)}, /*index=5*/f32[640,256]{1,0:T(8,128)S(1)}) custom-call(bf16[32,48,128]{2,1,0:T(8,128)(2,1)S(1)} %all-to-all-done.streams, f32[3,3,16]{2,1,0:T(4,128)S(1)} %copy-done.11, ...), custom_call_target="tpu_custom_call" | custom-call | tf_op jit(solution)/shard_map/front/pallas_call | solution.py:304
  53.5 1.5 %mixed_grad.1 = bf16[32,32,512]{2,1,0:T(8,128)(2,1)S(1)} custom-call(s32[6]{0:T(128)S(1)} %stack.57.place, bf16[4,512,128]{2,1,0:T(8,128)(2,1)S(1)} %pad_maximum_fusion.w_near, bf16[4,512,128]{2,1,0:T(8,128)(2,1)S(1)} %collective-permute-done.3.w_far, bf16[4,128,512]{2,1,0:T(8,128)(2,1)S(1)} %pad_maximum_fusion.1.g_near, ...), custom_call_target="tpu_custom_call", output_to_operand_aliasing={{}: (5, {})} | custom-call | tf_op jit(solution)/shard_map/mixed_grad/pallas_call | solution.py:319
  55.0 37.1 %all_to_all.15.mixed.upstream = bf16[32,32,512]{2,1,0:T(8,128)(2,1)S(1)} all-to-all(bf16[32,32,512]{2,1,0:T(8,128)(2,1)S(1)} %mixed_grad.1), channel_id=1, replica_groups=mesh['ctx'=32,'tp'=8] {'ctx'}, dimensions={0} | all-to-all | bytes 2097152 | tf_op jit(solution)/shard_map/all_to_all | solution.py:331
  92.1 3.0 %projections.1 = (bf16[4,128,512]{2,1,0:T(8,128)(2,1)S(1)}, bf16[4,128,512]{2,1,0:T(8,128)(2,1)}, bf16[4,512,128]{2,1,0:T(8,128)(2,1)S(1)}, bf16[4,512,128]{2,1,0:T(8,128)(2,1)S(1)}) custom-call(s32[6]{0:T(128)S(1)} %copy-done.14, bf16[32,32,512]{2,1,0:T(8,128)(2,1)S(1)} %all_to_all.15.mixed.upstream, bf16[4,512,128]{2,1,0:T(8,128)(2,1)S(1)} %pad_maximum_fusion.w_near, ...), custom_call_target="tpu_custom_call" | custom-call | tf_op jit(solution)/shard_map/projections/pallas_call | solution.py:333
  95.2 0.8 copy-done.3
  96.0 1.7 %collective-permute-start.9 = (bf16[4,128,512]{2,1,0:T(8,128)(2,1)}, bf16[4,128,512]{2,1,0:T(8,128)(2,1)S(1)}, u32[]{:S(2)}, u32[]{:S(2)}) collective-permute-start(bf16[4,128,512]{2,1,0:T(8,128)(2,1)} %get-tuple-element.18), channel_id=1, source_target_pairs={{0,1},{1,0},{2,3},{3,2},{4,5},{5,4},{6,7},{7,6},{8,9},{9,8},{10,11... | collective-permute-start | bytes 1572872 | tf_op jit(solution)/shard_map/ppermute | solution.py:267
  97.8 0.6 copy-done.16
  98.4 4.3 %rear.1 = (bf16[32,48,128]{2,1,0:T(8,128)(2,1)}, f32[16,4096]{1,0:T(8,128)}) custom-call(bf16[32,32,512]{2,1,0:T(8,128)(2,1)S(1)} %all_to_all.15.mixed.upstream, f32[3,3,16]{2,1,0:T(4,128)S(1)} %copy-done.12, f32[16]{0:T(128)S(1)} %copy-done.16, f32[640,256]{1,0:T(8,128)S(1)} %filter_spectrum.1.kernel, f32[640,256]{1,0:T(8,128)S(1)} %get-tuple-element.19.spectrum, ...), custom_call_target="tpu_custom_call" | custom-call | tf_op jit(solution)/shard_map/rear/pallas_call | solution.py:358
  102.8 3.8 %all-to-all-start.2 = ((bf16[32,48,128]{2,1,0:T(8,128)(2,1)}), bf16[32,48,128]{2,1,0:T(8,128)(2,1)S(1)}, u32[]{:S(2)}, u32[]{:S(2)}) async-start(bf16[32,48,128]{2,1,0:T(8,128)(2,1)} %get-tuple-element.24), calls=%async_computation.2 | async-start | bytes 786432 | tf_op jit(solution)/shard_map/all_to_all | solution.py:374
  106.6 0.1 collective-permute-start.14
  106.7 3.1 %collective-permute-done.9 = bf16[4,128,512]{2,1,0:T(8,128)(2,1)S(1)} collective-permute-done((bf16[4,128,512]{2,1,0:T(8,128)(2,1)}, bf16[4,128,512]{2,1,0:T(8,128)(2,1)S(1)}, u32[]{:S(2)}, u32[]{:S(2)}) %collective-permute-start.9) | collective-permute-done | bytes 524320 | tf_op jit(solution)/shard_map/ppermute | solution.py:267
  109.8 0.2 fusion.8
  110.0 1.3 collective-permute-start.10
  111.3 0.9 collective-permute-start.12
  112.3 2.0 %collective-permute-start.11 = (bf16[128,512]{1,0:T(8,128)(2,1)S(1)}, bf16[128,512]{1,0:T(8,128)(2,1)S(1)}, u32[]{:S(2)}, u32[]{:S(2)}) collective-permute-start(bf16[128,512]{1,0:T(8,128)(2,1)S(1)} %get-tuple-element.37), channel_id=1, source_target_pairs={{0,4},{1,5},{2,6},{3,7},{4,0},{5,1},{6,2},{7,3},{8,12},{9,13},{10,... | collective-permute-start | bytes 393224 | tf_op jit(solution)/shard_map/ppermute | solution.py:267
  114.2 0.1 fusion.9
  114.4 0.1 collective-permute-start.15
  114.5 1.5 %collective-permute-start.17 = (bf16[512,128]{1,0:T(8,128)(2,1)S(1)}, bf16[512,128]{1,0:T(8,128)(2,1)S(1)}, u32[]{:S(2)}, u32[]{:S(2)}) collective-permute-start(bf16[512,128]{1,0:T(8,128)(2,1)S(1)} %get-tuple-element.33), channel_id=1, source_target_pairs={{0,144},{8,152},{16,128},{24,136},{32,176},{40,184},{48,160},{56,1... | collective-permute-start | bytes 393224 | tf_op jit(solution)/shard_map/ppermute | solution.py:267
  116.0 3.5 %collective-permute-start.16 = (bf16[512,128]{1,0:T(8,128)(2,1)S(1)}, bf16[512,128]{1,0:T(8,128)(2,1)S(1)}, u32[]{:S(2)}, u32[]{:S(2)}) collective-permute-start(bf16[512,128]{1,0:T(8,128)(2,1)S(1)} %get-tuple-element.34), channel_id=1, source_target_pairs={{0,128},{8,136},{16,144},{24,152},{32,160},{40,168},{48,176},{56,1... | collective-permute-start | bytes 393224 | tf_op jit(solution)/shard_map/ppermute | solution.py:267
  119.5 0.1 fusion.7
  119.6 3.7 %collective-permute-start.13 = (bf16[128,512]{1,0:T(8,128)(2,1)S(1)}, bf16[128,512]{1,0:T(8,128)(2,1)S(1)}, u32[]{:S(2)}, u32[]{:S(2)}) collective-permute-start(bf16[128,512]{1,0:T(8,128)(2,1)S(1)} %fusion.7), channel_id=1, source_target_pairs={{0,0},{1,32},{2,64},{3,96},{4,4},{5,36},{6,68},{7,100},{8,8},{9,40... | collective-permute-start | bytes 393224 | tf_op jit(solution)/shard_map/ppermute | solution.py:277
  123.3 1.3 collective-permute-done.17
  124.6 1.0 collective-permute-done.16
  125.6 0.8 fusion.3
  126.4 0.8 copy.17
  127.1 6.8 %collective-permute-done.13 = bf16[128,512]{1,0:T(8,128)(2,1)S(1)} collective-permute-done((bf16[128,512]{1,0:T(8,128)(2,1)S(1)}, bf16[128,512]{1,0:T(8,128)(2,1)S(1)}, u32[]{:S(2)}, u32[]{:S(2)}) %collective-permute-start.13) | collective-permute-done | bytes 131104 | tf_op jit(solution)/shard_map/ppermute | solution.py:277
  133.9 0.7 copy.20
  (48 shorter events, 0.2 us)
Async XLA Ops:
  0.6 18.3 %collective-permute-start.4 = (bf16[128,512]{1,0:T(8,128)(2,1)}, bf16[128,512]{1,0:T(8,128)(2,1)S(1)}, u32[]{:S(2)}, u32[]{:S(2)}) collective-permute-start(bf16[128,512]{1,0:T(8,128)(2,1)} %param.16), channel_id=1, source_target_pairs={{0,0},{1,32},{2,64},{3,96},{4,4},{5,36},{6,68},{7,100},{8,8},{9,40... | collective-permute-start | bytes 393224 | tf_op jit(solution)/shard_map/ppermute | solution.py:277
  7.8 13.0 %collective-permute-start = (bf16[512,128]{1,0:T(8,128)(2,1)}, bf16[512,128]{1,0:T(8,128)(2,1)S(1)}, u32[]{:S(2)}, u32[]{:S(2)}) collective-permute-start(bf16[512,128]{1,0:T(8,128)(2,1)} %param.15), channel_id=1, source_target_pairs={{0,16},{8,24},{16,0},{24,8},{32,48},{40,56},{48,32},{56,40},{64,80... | collective-permute-start | bytes 393224 | tf_op jit(solution)/shard_map/ppermute | solution.py:267
  8.9 24.2 %collective-permute-start.2 = (bf16[512,128]{1,0:T(8,128)(2,1)}, bf16[512,128]{1,0:T(8,128)(2,1)S(1)}, u32[]{:S(2)}, u32[]{:S(2)}) collective-permute-start(bf16[512,128]{1,0:T(8,128)(2,1)} %param.15), channel_id=1, source_target_pairs={{0,144},{8,152},{16,128},{24,136},{32,176},{40,184},{48,160},{56,1... | collective-permute-start | bytes 393224 | tf_op jit(solution)/shard_map/ppermute | solution.py:267
  11.9 21.2 %collective-permute-start.1 = (bf16[512,128]{1,0:T(8,128)(2,1)}, bf16[512,128]{1,0:T(8,128)(2,1)S(1)}, u32[]{:S(2)}, u32[]{:S(2)}) collective-permute-start(bf16[512,128]{1,0:T(8,128)(2,1)} %param.15), channel_id=1, source_target_pairs={{0,128},{8,136},{16,144},{24,152},{32,160},{40,168},{48,176},{56,1... | collective-permute-start | bytes 393224 | tf_op jit(solution)/shard_map/ppermute | solution.py:267
  18.9 14.5 %collective-permute-start.7 = (bf16[128,512]{1,0:T(8,128)(2,1)S(1)}, bf16[128,512]{1,0:T(8,128)(2,1)S(1)}, u32[]{:S(2)}, u32[]{:S(2)}) collective-permute-start(bf16[128,512]{1,0:T(8,128)(2,1)S(1)} %collective-permute-done.4), channel_id=1, source_target_pairs={{0,6},{1,7},{2,4},{3,5},{4,2},{5,3},{6,0},{7,1},{8,14},{9,15},{10,... | collective-permute-start | bytes 393224 | tf_op jit(solution)/shard_map/ppermute | solution.py:267
  18.9 14.5 %collective-permute-start.6 = (bf16[128,512]{1,0:T(8,128)(2,1)S(1)}, bf16[128,512]{1,0:T(8,128)(2,1)S(1)}, u32[]{:S(2)}, u32[]{:S(2)}) collective-permute-start(bf16[128,512]{1,0:T(8,128)(2,1)S(1)} %collective-permute-done.4), channel_id=1, source_target_pairs={{0,4},{1,5},{2,6},{3,7},{4,0},{5,1},{6,2},{7,3},{8,12},{9,13},{10,... | collective-permute-start | bytes 393224 | tf_op jit(solution)/shard_map/ppermute | solution.py:267
  20.8 12.7 %collective-permute-start.5 = (bf16[128,512]{1,0:T(8,128)(2,1)S(1)}, bf16[128,512]{1,0:T(8,128)(2,1)S(1)}, u32[]{:S(2)}, u32[]{:S(2)}) collective-permute-start(bf16[128,512]{1,0:T(8,128)(2,1)S(1)} %collective-permute-done.4), channel_id=1, source_target_pairs={{0,2},{1,3},{2,0},{3,1},{4,6},{5,7},{6,4},{7,5},{8,10},{9,11},{10,... | collective-permute-start | bytes 393224 | tf_op jit(solution)/shard_map/ppermute | solution.py:267
  24.8 8.3 %copy-start.18 = (bf16[512,128]{1,0:T(8,128)(2,1)S(1)}, bf16[512,128]{1,0:T(8,128)(2,1)}, u32[]{:S(2)}) copy-start(bf16[512,128]{1,0:T(8,128)(2,1)} %param.15) | copy-start | bytes 393220
  24.8 24.9 %all-to-all-start = ((bf16[32,48,128]{2,1,0:T(8,128)(2,1)}), bf16[32,48,128]{2,1,0:T(8,128)(2,1)S(1)}, u32[]{:S(2)}, u32[]{:S(2)}) async-start(bf16[32,48,128]{2,1,0:T(8,128)(2,1)} %bitcast.16), calls=%async_computation | async-start | bytes 786432 | tf_op jit(solution)/shard_map/all_to_all | solution.py:292
  33.2 20.3 %collective-permute-start.3 = (bf16[4,512,128]{2,1,0:T(8,128)(2,1)S(1)}, bf16[4,512,128]{2,1,0:T(8,128)(2,1)S(1)}, u32[]{:S(2)}, u32[]{:S(2)}) collective-permute-start(bf16[4,512,128]{2,1,0:T(8,128)(2,1)S(1)} %pad_maximum_fusion.w_near), channel_id=1, source_target_pairs={{0,8},{8,0},{16,24},{24,16},{32,40},{40,32},{48,56},{56,48},{64,72... | collective-permute-start | bytes 1572872 | tf_op jit(solution)/shard_map/ppermute | solution.py:267
  33.4 1.1 copy-start
  33.5 1.1 copy-start.5
  33.5 1.1 copy-start.7
  33.6 20.0 %collective-permute-start.8 = (bf16[4,128,512]{2,1,0:T(8,128)(2,1)S(1)}, bf16[4,128,512]{2,1,0:T(8,128)(2,1)S(1)}, u32[]{:S(2)}, u32[]{:S(2)}) collective-permute-start(bf16[4,128,512]{2,1,0:T(8,128)(2,1)S(1)} %pad_maximum_fusion.1.g_near), channel_id=1, source_target_pairs={{0,1},{1,0},{2,3},{3,2},{4,5},{5,4},{6,7},{7,6},{8,9},{9,8},{10,11... | collective-permute-start | bytes 1572872 | tf_op jit(solution)/shard_map/ppermute | solution.py:267
  34.5 1.0 copy-start.9
  35.5 14.1 %copy-start.10 = (bf16[2,32,80]{2,1,0:T(8,128)(2,1)S(1)}, bf16[2,32,80]{2,1,0:T(8,128)(2,1)}, u32[]{:S(2)}) copy-start(bf16[2,32,80]{2,1,0:T(8,128)(2,1)} %constant.31.clone.last) | copy-start | bytes 30724
  36.4 13.2 %copy-start.11 = (f32[3,3,16]{2,1,0:T(4,128)S(1)}, f32[3,3,16]{2,1,0:T(4,128)}, u32[]{:S(2)}) copy-start(f32[3,3,16]{2,1,0:T(4,128)} %short_w.3) | copy-start | bytes 1732
  36.4 13.2 %copy-start.15 = (f32[16]{0:T(128)S(1)}, f32[16]{0:T(128)}, u32[]{:S(2)}) copy-start(f32[16]{0:T(128)} %skip.3) | copy-start | bytes 196
  36.5 17.0 %copy-start.13 = (s32[6]{0:T(128)}, s32[6]{0:T(128)S(1)}, u32[]{:S(2)}) copy-start(s32[6]{0:T(128)S(1)} %stack.57.place) | copy-start | bytes 76
  49.7 1.0 copy-start.1
  55.0 37.1 %copy-start.14 = (s32[6]{0:T(128)S(1)}, s32[6]{0:T(128)}, u32[]{:S(2)}) copy-start(s32[6]{0:T(128)} %copy-done.13) | copy-start | bytes 76
  92.1 5.6 %copy-start.2 = (bf16[2,256,256]{2,1,0:T(8,128)(2,1)S(1)}, bf16[2,256,256]{2,1,0:T(8,128)(2,1)}, u32[]{:S(2)}) copy-start(bf16[2,256,256]{2,1,0:T(8,128)(2,1)} %constant.30.clone.back) | copy-start | bytes 786436
  92.1 5.6 %copy-start.6 = (f32[2,40,128]{2,1,0:T(8,128)S(1)}, f32[2,40,128]{2,1,0:T(8,128)}, u32[]{:S(2)}) copy-start(f32[2,40,128]{2,1,0:T(8,128)} %constant.28.clone.twist) | copy-start | bytes 122884
  92.1 5.6 %copy-start.8 = (bf16[2,80,32]{2,1,0:T(8,128)(2,1)S(1)}, bf16[2,80,32]{2,1,0:T(8,128)(2,1)}, u32[]{:S(2)}) copy-start(bf16[2,80,32]{2,1,0:T(8,128)(2,1)} %constant.27.clone.first) | copy-start | bytes 30724
  95.2 0.8 copy-start.3
  96.0 6.7 %copy-start.17 = (bf16[4,512,128]{2,1,0:T(8,128)(2,1)}, bf16[4,512,128]{2,1,0:T(8,128)(2,1)S(1)}, u32[]{:S(2)}) copy-start(bf16[4,512,128]{2,1,0:T(8,128)(2,1)S(1)} %get-tuple-element.27) | copy-start | bytes 1572868
  96.0 1.7 %copy-start.12 = (f32[3,3,16]{2,1,0:T(4,128)S(1)}, f32[3,3,16]{2,1,0:T(4,128)}, u32[]{:S(2)}) copy-start(f32[3,3,16]{2,1,0:T(4,128)} %short_w.3) | copy-start | bytes 1732
  96.0 13.8 %collective-permute-start.9 = (bf16[4,128,512]{2,1,0:T(8,128)(2,1)}, bf16[4,128,512]{2,1,0:T(8,128)(2,1)S(1)}, u32[]{:S(2)}, u32[]{:S(2)}) collective-permute-start(bf16[4,128,512]{2,1,0:T(8,128)(2,1)} %get-tuple-element.18), channel_id=1, source_target_pairs={{0,1},{1,0},{2,3},{3,2},{4,5},{5,4},{6,7},{7,6},{8,9},{9,8},{10,11... | collective-permute-start | bytes 1572872 | tf_op jit(solution)/shard_map/ppermute | solution.py:267
  97.7 0.7 copy-start.16
  102.8 7.1 %copy-start.4 = (bf16[4,128,512]{2,1,0:T(8,128)(2,1)S(1)}, bf16[4,128,512]{2,1,0:T(8,128)(2,1)}, u32[]{:S(2)}) copy-start(bf16[4,128,512]{2,1,0:T(8,128)(2,1)} %copy-done.3) | copy-start | bytes 1572868
  102.8 23.6 %all-to-all-start.2 = ((bf16[32,48,128]{2,1,0:T(8,128)(2,1)}), bf16[32,48,128]{2,1,0:T(8,128)(2,1)S(1)}, u32[]{:S(2)}, u32[]{:S(2)}) async-start(bf16[32,48,128]{2,1,0:T(8,128)(2,1)} %get-tuple-element.24), calls=%async_computation.2 | async-start | bytes 786432 | tf_op jit(solution)/shard_map/all_to_all | solution.py:374
  106.6 7.7 %collective-permute-start.14 = (bf16[4,512,128]{2,1,0:T(8,128)(2,1)}, bf16[4,512,128]{2,1,0:T(8,128)(2,1)S(1)}, u32[]{:S(2)}, u32[]{:S(2)}) collective-permute-start(bf16[4,512,128]{2,1,0:T(8,128)(2,1)} %copy-done.17), channel_id=1, source_target_pairs={{0,8},{8,0},{16,24},{24,16},{32,40},{40,32},{48,56},{56,48},{64,72... | collective-permute-start | bytes 1572872 | tf_op jit(solution)/shard_map/ppermute | solution.py:267
  110.0 6.0 %collective-permute-start.10 = (bf16[128,512]{1,0:T(8,128)(2,1)S(1)}, bf16[128,512]{1,0:T(8,128)(2,1)S(1)}, u32[]{:S(2)}, u32[]{:S(2)}) collective-permute-start(bf16[128,512]{1,0:T(8,128)(2,1)S(1)} %get-tuple-element.35), channel_id=1, source_target_pairs={{0,2},{1,3},{2,0},{3,1},{4,6},{5,7},{6,4},{7,5},{8,10},{9,11},{10,... | collective-permute-start | bytes 393224 | tf_op jit(solution)/shard_map/ppermute | solution.py:267
  111.3 8.2 %collective-permute-start.12 = (bf16[128,512]{1,0:T(8,128)(2,1)S(1)}, bf16[128,512]{1,0:T(8,128)(2,1)S(1)}, u32[]{:S(2)}, u32[]{:S(2)}) collective-permute-start(bf16[128,512]{1,0:T(8,128)(2,1)S(1)} %get-tuple-element.36), channel_id=1, source_target_pairs={{0,6},{1,7},{2,4},{3,5},{4,2},{5,3},{6,0},{7,1},{8,14},{9,15},{10,... | collective-permute-start | bytes 393224 | tf_op jit(solution)/shard_map/ppermute | solution.py:267
  112.3 7.2 %collective-permute-start.11 = (bf16[128,512]{1,0:T(8,128)(2,1)S(1)}, bf16[128,512]{1,0:T(8,128)(2,1)S(1)}, u32[]{:S(2)}, u32[]{:S(2)}) collective-permute-start(bf16[128,512]{1,0:T(8,128)(2,1)S(1)} %get-tuple-element.37), channel_id=1, source_target_pairs={{0,4},{1,5},{2,6},{3,7},{4,0},{5,1},{6,2},{7,3},{8,12},{9,13},{10,... | collective-permute-start | bytes 393224 | tf_op jit(solution)/shard_map/ppermute | solution.py:267
  114.4 8.9 %collective-permute-start.15 = (bf16[512,128]{1,0:T(8,128)(2,1)S(1)}, bf16[512,128]{1,0:T(8,128)(2,1)S(1)}, u32[]{:S(2)}, u32[]{:S(2)}) collective-permute-start(bf16[512,128]{1,0:T(8,128)(2,1)S(1)} %get-tuple-element.32), channel_id=1, source_target_pairs={{0,16},{8,24},{16,0},{24,8},{32,48},{40,56},{48,32},{56,40},{64,80... | collective-permute-start | bytes 393224 | tf_op jit(solution)/shard_map/ppermute | solution.py:267
  114.5 10.1 %collective-permute-start.17 = (bf16[512,128]{1,0:T(8,128)(2,1)S(1)}, bf16[512,128]{1,0:T(8,128)(2,1)S(1)}, u32[]{:S(2)}, u32[]{:S(2)}) collective-permute-start(bf16[512,128]{1,0:T(8,128)(2,1)S(1)} %get-tuple-element.33), channel_id=1, source_target_pairs={{0,144},{8,152},{16,128},{24,136},{32,176},{40,184},{48,160},{56,1... | collective-permute-start | bytes 393224 | tf_op jit(solution)/shard_map/ppermute | solution.py:267
  116.0 9.6 %collective-permute-start.16 = (bf16[512,128]{1,0:T(8,128)(2,1)S(1)}, bf16[512,128]{1,0:T(8,128)(2,1)S(1)}, u32[]{:S(2)}, u32[]{:S(2)}) collective-permute-start(bf16[512,128]{1,0:T(8,128)(2,1)S(1)} %get-tuple-element.34), channel_id=1, source_target_pairs={{0,128},{8,136},{16,144},{24,152},{32,160},{40,168},{48,176},{56,1... | collective-permute-start | bytes 393224 | tf_op jit(solution)/shard_map/ppermute | solution.py:267
  119.6 14.3 %collective-permute-start.13 = (bf16[128,512]{1,0:T(8,128)(2,1)S(1)}, bf16[128,512]{1,0:T(8,128)(2,1)S(1)}, u32[]{:S(2)}, u32[]{:S(2)}) collective-permute-start(bf16[128,512]{1,0:T(8,128)(2,1)S(1)} %fusion.7), channel_id=1, source_target_pairs={{0,0},{1,32},{2,64},{3,96},{4,4},{5,36},{6,68},{7,100},{8,8},{9,40... | collective-permute-start | bytes 393224 | tf_op jit(solution)/shard_map/ppermute | solution.py:277
where the time goes:
time: 136 us; the launch traced here: 135 us
  starting transfers between devices  44.5 us (33%)
  blocking collectives  37.1 us (27%)
  waiting for transfers between devices  31.3 us (23%)
  Pallas kernels  12.7 us (9%)
  local copies, waits for them, and re-layouts  6.76 us (5%)
    all_to_all x1, blocking collectives, shards(): joint = lax.all_to_all(buffer, 'ctx', 0, 0)  37.1 us
    ppermute x16, starting transfers between devices, flip(): return lax.ppermute(values, axis, [(i, i ^ mask) for i in range(size)])  21.5 us
    all_to_all x1, waiting for transfers between devices, shards(): streams = lax.all_to_all(sent, 'ctx', 0, 0)  13.1 us
    ppermute x2, waiting for transfers between devices, exchange(): return lax.ppermute(values, ('ctx', 'tp'), pairs)  12.8 us
    ppermute x2, starting transfers between devices, exchange(): return lax.ppermute(values, ('ctx', 'tp'), pairs)  10.9 us
    all_to_all x1, starting transfers between devices, shards(): streams = lax.all_to_all(sent, 'ctx', 0, 0)  8.29 us
    ppermute x16, waiting for transfers between devices, flip(): return lax.ppermute(values, axis, [(i, i ^ mask) for i in range(size)])  5.43 us
    pallas_call x1, Pallas kernels, shards(): pl.pallas_call(rear_kernel, out_shape=[half(SH, 3 * CH, LN), flat(CH, SEQ...  4.35 us
  transfers between devices with their start and end apart: 20, of which 6 were waited for; matrix products, arithmetic and copies ran while one was open for 3% of the time, Pallas kernels for 6%

commit v1 on v0

--- a/solution.py
+++ b/solution.py
@@ -40,10 +40,9 @@
     two = 2 * math.pi * b[:, None] * b[None, :] / 128
     c2, s2 = np.cos(two), np.sin(two)
     second = np.block([[c2, -s2], [s2, c2]])
-    back = np.block([[c2, s2], [-s2, c2]])
     weight = np.where((d == 0) | (d == 32), 1.0, 2.0) * live / 8192
     last = np.concatenate([(np.cos(one) * weight).T, (-np.sin(one) * weight).T], axis=1)
-    return split(first), twist, split(second), split(back), split(last)
+    return split(first), twist, split(second), split(last)
 
 
 def parts(values):
@@ -61,9 +60,14 @@
     return dot(table[0], high) + dot(table[0], low) + dot(table[1], high)
 
 
-def table_right(values, table):
+def table_right(values, table, side):
+    def times_table(piece, k):
+        return lax.dot_general(
+            piece, table[k], (((1,), (side,)), ((), ())), preferred_element_type=F32
+        )
+
     high, low = parts(values)
-    return dot(high, table[0]) + dot(low, table[0]) + dot(high, table[1])
+    return times_table(high, 0) + times_table(low, 0) + times_table(high, 1)
 
 
 def column(c):
@@ -77,11 +81,11 @@
         real, imag = grid[:HALF, column(c)], grid[HALF:, column(c)]
         work[c * HALF : (c + 1) * HALF, :LN] = real * cosine + imag * sine
         work[c * HALF : (c + 1) * HALF, LN:] = imag * cosine - real * sine
-    return table_right(work[...], second)
-
-
-def inverse(spectrum, twist, back, last):
-    grid = table_right(spectrum, back)
+    return table_right(work[...], second, 0)
+
+
+def inverse(spectrum, twist, second, last):
+    grid = table_right(spectrum, second, 1)
     cosine, sine = twist[0], twist[1]
     columns = []
     for c in range(CH):
@@ -127,7 +131,7 @@
 
 
 def front_kernel(
-    streams, short_w, skip, kernel, first, twist, second, back, last,
+    streams, short_w, skip, kernel, first, twist, second, last,
     outgoing, query, left, right, signal, spectrum, rows, work, packed,
 ):
     lane, row = lane_row()
@@ -148,7 +152,7 @@
         gated.append((conv[1] * conv[2]).astype(BF16).astype(F32))
     own = forward(jnp.concatenate(gated, axis=1), first, twist, second, work)
     spectrum[...] = own
-    total = inverse(times(kernel[...], own, False), twist, back, last)
+    total = inverse(times(kernel[...], own, False), twist, second, last)
     for c in range(CH):
         value = total[:, column(c)] + skip[c] * gated[c]
         signal[:, column(c)] = value
@@ -164,7 +168,7 @@
 
 def rear_kernel(
     upstream, short_w, skip, kernel, spectrum, query, left, right, signal,
-    first, twist, second, back, last,
+    first, twist, second, last,
     outgoing, grad_filters, rows, work, packed, turned,
 ):
     lane, row = lane_row()
@@ -189,14 +193,14 @@
         grad_signal.append(up * query[:, column(c)])
         emit(0, c, (up * signal[:, column(c)]).astype(BF16).astype(F32))
     own = forward(jnp.concatenate(grad_signal, axis=1), first, twist, second, work)
-    through = inverse(times(kernel[...], own, True), twist, back, last)
+    through = inverse(times(kernel[...], own, True), twist, second, last)
     for c in range(CH):
         grad = (through[:, column(c)] + skip[c] * grad_signal[c]).astype(BF16).astype(F32)
         emit(1, c, grad * right[:, column(c)])
         emit(2, c, grad * left[:, column(c)])
     for j in range(SH):
         outgoing[j] = packed[j * 48 : (j + 1) * 48, :].astype(BF16)
-    taps = inverse(times(spectrum[...], own, True), twist, back, last)
+    taps = inverse(times(spectrum[...], own, True), twist, second, last)
     for c in range(CH):
         turned[c * SH : (c + 1) * SH, :] = taps[:, column(c)] * (SEQ**-0.5)
     for a in range(SH):
@@ -278,18 +282,20 @@
 
 
 def shards(qkv, short_w, filters, skip, w_out, grad_out):
-    first, twist, second, back, last = [jnp.asarray(t) for t in tables()]
+    first, twist, second, last = [jnp.asarray(t) for t in tables()]
     j, i = lax.axis_index("ctx"), lax.axis_index("tp")
     place = jnp.stack([j >> 4, (j >> 1) & 1, j & 1, i >> 2, (i >> 1) & 1, i & 1]).astype(jnp.int32)
 
-    w_near = jnp.stack([w_out] + [flip(w_out, "ctx", 32, m) for m in (2, 16, 18)])
+    sent = qkv.reshape(3, SH, CH, LN).transpose(1, 0, 2, 3).reshape(SH, 3 * CH, LN)
+    tile = exchange(grad_out)
+    w_got = [flip(w_out, "ctx", 32, m) for m in (2, 16, 18)]
+    sent, tile, place, *w_got = lax.optimization_barrier((sent, tile, place, *w_got))
+    streams = lax.all_to_all(sent, "ctx", 0, 0)
+    near = jnp.stack([tile] + [flip(tile, "tp", 8, m) for m in (2, 4, 6)])
+    tiles = [near, flip(near, "tp", 8, 1)]
+    w_near = jnp.stack([w_out, *w_got])
+    streams, _ = lax.optimization_barrier((streams, near))
     w_far = flip(w_near, "ctx", 32, 1)
-    tile = exchange(grad_out)
-    g_near = jnp.stack([tile] + [flip(tile, "tp", 8, m) for m in (2, 4, 6)])
-    g_far = flip(g_near, "tp", 8, 1)
-
-    sent = qkv.reshape(3, SH, CH, LN).transpose(1, 0, 2, 3).reshape(SH, 3 * CH, LN)
-    streams = lax.all_to_all(sent, "ctx", 0, 0)
 
     kernel = pl.pallas_call(
         filter_kernel,
@@ -304,7 +310,7 @@
     buffer, query, left, right, signal, spectrum = pl.pallas_call(
         front_kernel,
         out_shape=[half(SH, 2 * CH, 512)] + [flat(SH, CH * LN)] * 4 + [flat(CH * HALF, 2 * LN)],
-        in_specs=[VM, SM, SM] + [VM] * 6,
+        in_specs=[VM, SM, SM] + [VM] * 5,
         out_specs=[pl.BlockSpec((SH, CH, 512), lambda g: (0, 0, 0))] + [VM] * 5,
         scratch_shapes=[
             pltpu.VMEM((SH * 48, LN), F32),
@@ -314,7 +320,7 @@
         grid=(1,),
         compiler_params=PARAMS,
         name="front",
-    )(streams, short_w, skip, kernel, first, twist, second, back, last)
+    )(streams, short_w, skip, kernel, first, twist, second, last)
 
     buffer = pl.pallas_call(
         mixed_grad_kernel,
@@ -326,7 +332,7 @@
         grid=(1,),
         compiler_params=PARAMS,
         name="mixed_grad",
-    )(place, w_near, w_far, g_near, g_far, buffer)
+    )(place, w_near, w_far, *tiles, buffer)
 
     joint = lax.all_to_all(buffer, "ctx", 0, 0)
 
@@ -339,7 +345,7 @@
         grid=(1,),
         compiler_params=PARAMS,
         name="projections",
-    )(place, joint, w_near, w_far, g_near, g_far)
+    )(place, joint, w_near, w_far, *tiles)
 
     o_sum = o_near.astype(F32) + flip(o_far, "tp", 8, 1).astype(F32)
     o_sent = o_sum.astype(BF16)
@@ -358,7 +364,7 @@
     grads, grad_filters = pl.pallas_call(
         rear_kernel,
         out_shape=[half(SH, 3 * CH, LN), flat(CH, SEQ)],
-        in_specs=[pl.BlockSpec((SH, CH, 512), lambda g: (0, 1, 0)), SM, SM] + [VM] * 11,
+        in_specs=[pl.BlockSpec((SH, CH, 512), lambda g: (0, 1, 0)), SM, SM] + [VM] * 10,
         out_specs=[VM, VM],
         scratch_shapes=[
             pltpu.VMEM((SH * CH, LN), F32),
@@ -369,7 +375,7 @@
         grid=(1,),
         compiler_params=PARAMS,
         name="rear",
-    )(joint, short_w, skip, kernel, spectrum, query, left, right, signal, first, twist, second, back, last)
+    )(joint, short_w, skip, kernel, spectrum, query, left, right, signal, first, twist, second, last)
 
     returned = lax.all_to_all(grads, "ctx", 0, 0)
     grad_qkv = returned.reshape(SH, 3, CH, LN).transpose(1, 0, 2, 3).reshape(3, SH * CH, LN)

time: 136 us -> 133 us (0.978)
  local copies, waits for them, and re-layouts: 6.76 us -> 4.06 us
    unnamed x39 -> x35, local copies, waits for them, and re-layouts: 4.08 us -> 1.38 us
    ppermute x2, waiting for transfers between devices: 12.8 us -> 11 us  [exchange(): return lax.ppermute(values, ('ctx', 'tp'), pairs)]
  transfers between devices with their start and end apart: 20 -> 20, of which waited for: 6 -> 7; matrix products, arithmetic and copies ran while one was open for 3% -> 3% of each run, Pallas kernels for 6% -> 6%
where the time goes in v1:
time: 133 us
  starting transfers between devices  44.5 us (33%)
  blocking collectives  38.3 us (29%)
  waiting for transfers between devices  31 us (23%)
  Pallas kernels  12.5 us (9%)
  local copies, waits for them, and re-layouts  4.06 us (3%)
    all_to_all x1, blocking collectives, shards(): joint = lax.all_to_all(buffer, 'ctx', 0, 0)  38.3 us
    ppermute x16, starting transfers between devices, flip(): return lax.ppermute(values, axis, [(i, i ^ mask) for i in range(size)])  21.7 us
    all_to_all x1, waiting for transfers between devices, shards(): streams = lax.all_to_all(sent, 'ctx', 0, 0)  13.7 us
    ppermute x2, waiting for transfers between devices, exchange(): return lax.ppermute(values, ('ctx', 'tp'), pairs)  11 us
    ppermute x2, starting transfers between devices, exchange(): return lax.ppermute(values, ('ctx', 'tp'), pairs)  10.6 us
    all_to_all x1, starting transfers between devices, shards(): streams = lax.all_to_all(sent, 'ctx', 0, 0)  8.39 us
    ppermute x16, waiting for transfers between devices, flip(): return lax.ppermute(values, axis, [(i, i ^ mask) for i in range(size)])  6.33 us
    pallas_call x1, Pallas kernels, shards(): pl.pallas_call(rear_kernel, out_shape=[half(SH, 3 * CH, LN), flat(CH, SEQ...  4.21 us
  transfers between devices with their start and end apart: 20, of which 7 were waited for; matrix products, arithmetic and copies ran while one was open for 3% of the time, Pallas kernels for 6%

profile of v1, /device:TPU:42, one launch (start us, length us, event | category | flops | bytes accessed | tf_op | source)
XLA Modules:
  0.0 132.6 jit_solution(15030344783857306877)
XLA Ops:
  0.6 7.2 %collective-permute-start = (bf16[128,512]{1,0:T(8,128)(2,1)}, bf16[128,512]{1,0:T(8,128)(2,1)S(1)}, u32[]{:S(2)}, u32[]{:S(2)}) collective-permute-start(bf16[128,512]{1,0:T(8,128)(2,1)} %param.15), channel_id=1, source_target_pairs={{0,0},{1,32},{2,64},{3,96},{4,4},{5,36},{6,68},{7,100},{8,8},{9,40... | collective-permute-start | bytes 393224 | tf_op jit(solution)/shard_map/ppermute | solution.py:281
  7.8 2.7 %collective-permute-start.2 = (bf16[512,128]{1,0:T(8,128)(2,1)}, bf16[512,128]{1,0:T(8,128)(2,1)S(1)}, u32[]{:S(2)}, u32[]{:S(2)}) collective-permute-start(bf16[512,128]{1,0:T(8,128)(2,1)} %param.14), channel_id=1, source_target_pairs={{0,128},{8,136},{16,144},{24,152},{32,160},{40,168},{48,176},{56,1... | collective-permute-start | bytes 393224 | tf_op jit(solution)/shard_map/ppermute | solution.py:271
  10.5 1.0 collective-permute-start.1
  11.5 1.4 %collective-permute-start.3 = (bf16[512,128]{1,0:T(8,128)(2,1)}, bf16[512,128]{1,0:T(8,128)(2,1)S(1)}, u32[]{:S(2)}, u32[]{:S(2)}) collective-permute-start(bf16[512,128]{1,0:T(8,128)(2,1)} %param.14), channel_id=1, source_target_pairs={{0,144},{8,152},{16,128},{24,136},{32,176},{40,184},{48,160},{56,1... | collective-permute-start | bytes 393224 | tf_op jit(solution)/shard_map/ppermute | solution.py:271
  12.9 1.8 %copy.15 = bf16[3,32,16,128]{3,2,0,1:T(8,128)(2,1)} copy(bf16[3,32,16,128]{3,2,1,0:T(8,128)(2,1)} %bitcast.55) | data formatting | bytes 786432 | tf_op jit(solution)/shard_map/reshape | solution.py:289
  14.7 0.1 stack.57.place
  14.7 4.1 %collective-permute-done = bf16[128,512]{1,0:T(8,128)(2,1)S(1)} collective-permute-done((bf16[128,512]{1,0:T(8,128)(2,1)}, bf16[128,512]{1,0:T(8,128)(2,1)S(1)}, u32[]{:S(2)}, u32[]{:S(2)}) %collective-permute-start) | collective-permute-done | bytes 131104 | tf_op jit(solution)/shard_map/ppermute | solution.py:281
  18.9 0.4 collective-permute-done.3
  19.3 1.9 %collective-permute-start.7 = (bf16[128,512]{1,0:T(8,128)(2,1)S(1)}, bf16[128,512]{1,0:T(8,128)(2,1)S(1)}, u32[]{:S(2)}, u32[]{:S(2)}) collective-permute-start(bf16[128,512]{1,0:T(8,128)(2,1)S(1)} %collective-permute-done), channel_id=1, source_target_pairs={{0,6},{1,7},{2,4},{3,5},{4,2},{5,3},{6,0},{7,1},{8,14},{9,15},{10,... | collective-permute-start | bytes 393224 | tf_op jit(solution)/shard_map/ppermute | solution.py:271
  21.2 1.1 collective-permute-start.6
  22.3 1.1 collective-permute-start.5
  23.4 8.4 %all-to-all-start = ((bf16[32,48,128]{2,1,0:T(8,128)(2,1)}), bf16[32,48,128]{2,1,0:T(8,128)(2,1)S(1)}, u32[]{:S(2)}, u32[]{:S(2)}) async-start(bf16[32,48,128]{2,1,0:T(8,128)(2,1)} %bitcast.2), calls=%async_computation | async-start | bytes 786432 | tf_op jit(solution)/shard_map/all_to_all | solution.py:293
  31.8 0.1 pad_maximum_fusion.w_near
  31.9 0.2 collective-permute-start.4
  32.2 0.0 copy-start
  32.2 0.0 copy-start.3
  32.2 0.0 copy-start.5
  32.2 0.1 pad_maximum_fusion.1.g_near
  32.3 0.0 copy-start.8
  32.3 1.4 %collective-permute-start.8 = (bf16[4,128,512]{2,1,0:T(8,128)(2,1)S(1)}, bf16[4,128,512]{2,1,0:T(8,128)(2,1)S(1)}, u32[]{:S(2)}, u32[]{:S(2)}) collective-permute-start(bf16[4,128,512]{2,1,0:T(8,128)(2,1)S(1)} %pad_maximum_fusion.1.g_near), channel_id=1, source_target_pairs={{0,1},{1,0},{2,3},{3,2},{4,5},{5,4},{6,7},{7,6},{8,9},{9,8},{10,11... | collective-permute-start | bytes 1572872 | tf_op jit(solution)/shard_map/ppermute | solution.py:271
  33.7 0.9 filter_spectrum.1.kernel
  34.6 13.7 %all-to-all-done.streams = bf16[32,48,128]{2,1,0:T(8,128)(2,1)S(1)} async-done(((bf16[32,48,128]{2,1,0:T(8,128)(2,1)}), bf16[32,48,128]{2,1,0:T(8,128)(2,1)S(1)}, u32[]{:S(2)}, u32[]{:S(2)}) %all-to-all-start) | async-done | bytes 393248 | tf_op jit(solution)/shard_map/all_to_all | solution.py:293
  48.4 2.9 %front.1 = (bf16[32,32,512]{2,1,0:T(8,128)(2,1)S(1)}, f32[32,2048]{1,0:T(8,128)S(1)}, f32[32,2048]{1,0:T(8,128)S(1)}, f32[32,2048]{1,0:T(8,128)S(1)}, f32[32,2048]{1,0:T(8,128)S(1)}, /*index=5*/f32[640,256]{1,0:T(8,128)S(1)}) custom-call(bf16[32,48,128]{2,1,0:T(8,128)(2,1)S(1)} %all-to-all-done.streams, f32[3,3,16]{2,1,0:T(4,128)S(1)} %copy-done.9, ...), custom_call_target="tpu_custom_call" | custom-call | tf_op jit(solution)/shard_map/front/pallas_call | solution.py:310
  51.3 1.5 %mixed_grad.1 = bf16[32,32,512]{2,1,0:T(8,128)(2,1)S(1)} custom-call(s32[6]{0:T(128)S(1)} %stack.57.place, bf16[4,512,128]{2,1,0:T(8,128)(2,1)S(1)} %pad_maximum_fusion.w_near, bf16[4,512,128]{2,1,0:T(8,128)(2,1)S(1)} %collective-permute-done.4.w_far, bf16[4,128,512]{2,1,0:T(8,128)(2,1)S(1)} %pad_maximum_fusion.1.g_near, ...), custom_call_target="tpu_custom_call", output_to_operand_aliasing={{}: (5, {})} | custom-call | tf_op jit(solution)/shard_map/mixed_grad/pallas_call | solution.py:325
  52.8 38.3 %all_to_all.15.mixed.upstream = bf16[32,32,512]{2,1,0:T(8,128)(2,1)S(1)} all-to-all(bf16[32,32,512]{2,1,0:T(8,128)(2,1)S(1)} %mixed_grad.1), channel_id=1, replica_groups=mesh['ctx'=32,'tp'=8] {'ctx'}, dimensions={0} | all-to-all | bytes 2097152 | tf_op jit(solution)/shard_map/all_to_all | solution.py:337
  91.1 3.0 %projections.1 = (bf16[4,128,512]{2,1,0:T(8,128)(2,1)S(1)}, bf16[4,128,512]{2,1,0:T(8,128)(2,1)}, bf16[4,512,128]{2,1,0:T(8,128)(2,1)S(1)}, bf16[4,512,128]{2,1,0:T(8,128)(2,1)S(1)}) custom-call(s32[6]{0:T(128)S(1)} %copy-done.12, bf16[32,32,512]{2,1,0:T(8,128)(2,1)S(1)} %all_to_all.15.mixed.upstream, bf16[4,512,128]{2,1,0:T(8,128)(2,1)S(1)} %pad_maximum_fusion.w_near, ...), custom_call_target="tpu_custom_call" | custom-call | tf_op jit(solution)/shard_map/projections/pallas_call | solution.py:339
  94.2 1.5 %collective-permute-start.9 = (bf16[4,128,512]{2,1,0:T(8,128)(2,1)}, bf16[4,128,512]{2,1,0:T(8,128)(2,1)S(1)}, u32[]{:S(2)}, u32[]{:S(2)}) collective-permute-start(bf16[4,128,512]{2,1,0:T(8,128)(2,1)} %get-tuple-element.32), channel_id=1, source_target_pairs={{0,1},{1,0},{2,3},{3,2},{4,5},{5,4},{6,7},{7,6},{8,9},{9,8},{10,11... | collective-permute-start | bytes 1572872 | tf_op jit(solution)/shard_map/ppermute | solution.py:271
  95.7 0.6 copy-done.14
  96.3 4.2 %rear.1 = (bf16[32,48,128]{2,1,0:T(8,128)(2,1)}, f32[16,4096]{1,0:T(8,128)}) custom-call(bf16[32,32,512]{2,1,0:T(8,128)(2,1)S(1)} %all_to_all.15.mixed.upstream, f32[3,3,16]{2,1,0:T(4,128)S(1)} %copy-done.10, f32[16]{0:T(128)S(1)} %copy-done.14, f32[640,256]{1,0:T(8,128)S(1)} %filter_spectrum.1.kernel, f32[640,256]{1,0:T(8,128)S(1)} %get-tuple-element.33.spectrum, ...), custom_call_target="tpu_custom_call" | custom-call | tf_op jit(solution)/shard_map/rear/pallas_call | solution.py:364
  100.6 3.8 %all-to-all-start.2 = ((bf16[32,48,128]{2,1,0:T(8,128)(2,1)}), bf16[32,48,128]{2,1,0:T(8,128)(2,1)S(1)}, u32[]{:S(2)}, u32[]{:S(2)}) async-start(bf16[32,48,128]{2,1,0:T(8,128)(2,1)} %get-tuple-element.38), calls=%async_computation.2 | async-start | bytes 786432 | tf_op jit(solution)/shard_map/all_to_all | solution.py:380
  104.4 0.1 collective-permute-start.14
  104.5 3.5 %collective-permute-done.9 = bf16[4,128,512]{2,1,0:T(8,128)(2,1)S(1)} collective-permute-done((bf16[4,128,512]{2,1,0:T(8,128)(2,1)}, bf16[4,128,512]{2,1,0:T(8,128)(2,1)S(1)}, u32[]{:S(2)}, u32[]{:S(2)}) %collective-permute-start.9) | collective-permute-done | bytes 524320 | tf_op jit(solution)/shard_map/ppermute | solution.py:271
  108.0 0.2 fusion.8
  108.2 0.6 collective-permute-start.10
  108.8 2.3 %collective-permute-start.12 = (bf16[128,512]{1,0:T(8,128)(2,1)S(1)}, bf16[128,512]{1,0:T(8,128)(2,1)S(1)}, u32[]{:S(2)}, u32[]{:S(2)}) collective-permute-start(bf16[128,512]{1,0:T(8,128)(2,1)S(1)} %get-tuple-element.50), channel_id=1, source_target_pairs={{0,6},{1,7},{2,4},{3,5},{4,2},{5,3},{6,0},{7,1},{8,14},{9,15},{10,... | collective-permute-start | bytes 393224 | tf_op jit(solution)/shard_map/ppermute | solution.py:271
  111.1 1.3 collective-permute-start.11
  112.4 0.1 fusion.9
  112.5 0.1 collective-permute-start.15
  112.6 1.5 %collective-permute-start.17 = (bf16[512,128]{1,0:T(8,128)(2,1)S(1)}, bf16[512,128]{1,0:T(8,128)(2,1)S(1)}, u32[]{:S(2)}, u32[]{:S(2)}) collective-permute-start(bf16[512,128]{1,0:T(8,128)(2,1)S(1)} %get-tuple-element.47), channel_id=1, source_target_pairs={{0,144},{8,152},{16,128},{24,136},{32,176},{40,184},{48,160},{56,1... | collective-permute-start | bytes 393224 | tf_op jit(solution)/shard_map/ppermute | solution.py:271
  114.2 3.5 %collective-permute-start.16 = (bf16[512,128]{1,0:T(8,128)(2,1)S(1)}, bf16[512,128]{1,0:T(8,128)(2,1)S(1)}, u32[]{:S(2)}, u32[]{:S(2)}) collective-permute-start(bf16[512,128]{1,0:T(8,128)(2,1)S(1)} %get-tuple-element.48), channel_id=1, source_target_pairs={{0,128},{8,136},{16,144},{24,152},{32,160},{40,168},{48,176},{56,1... | collective-permute-start | bytes 393224 | tf_op jit(solution)/shard_map/ppermute | solution.py:271
  117.6 0.1 fusion.7
  117.7 3.5 %collective-permute-start.13 = (bf16[128,512]{1,0:T(8,128)(2,1)S(1)}, bf16[128,512]{1,0:T(8,128)(2,1)S(1)}, u32[]{:S(2)}, u32[]{:S(2)}) collective-permute-start(bf16[128,512]{1,0:T(8,128)(2,1)S(1)} %fusion.7), channel_id=1, source_target_pairs={{0,0},{1,32},{2,64},{3,96},{4,4},{5,36},{6,68},{7,100},{8,8},{9,40... | collective-permute-start | bytes 393224 | tf_op jit(solution)/shard_map/ppermute | solution.py:281
  121.2 1.2 collective-permute-done.17
  122.4 1.2 collective-permute-done.16
  123.6 0.8 fusion.3
  124.3 0.8 copy.16
  125.1 6.8 %collective-permute-done.13 = bf16[128,512]{1,0:T(8,128)(2,1)S(1)} collective-permute-done((bf16[128,512]{1,0:T(8,128)(2,1)S(1)}, bf16[128,512]{1,0:T(8,128)(2,1)S(1)}, u32[]{:S(2)}, u32[]{:S(2)}) %collective-permute-start.13) | collective-permute-done | bytes 131104 | tf_op jit(solution)/shard_map/ppermute | solution.py:281
  131.9 0.7 copy.19
  (44 shorter events, 0.2 us)
Async XLA Ops:
  0.6 18.3 %collective-permute-start = (bf16[128,512]{1,0:T(8,128)(2,1)}, bf16[128,512]{1,0:T(8,128)(2,1)S(1)}, u32[]{:S(2)}, u32[]{:S(2)}) collective-permute-start(bf16[128,512]{1,0:T(8,128)(2,1)} %param.15), channel_id=1, source_target_pairs={{0,0},{1,32},{2,64},{3,96},{4,4},{5,36},{6,68},{7,100},{8,8},{9,40... | collective-permute-start | bytes 393224 | tf_op jit(solution)/shard_map/ppermute | solution.py:281
  7.8 11.1 %collective-permute-start.2 = (bf16[512,128]{1,0:T(8,128)(2,1)}, bf16[512,128]{1,0:T(8,128)(2,1)S(1)}, u32[]{:S(2)}, u32[]{:S(2)}) collective-permute-start(bf16[512,128]{1,0:T(8,128)(2,1)} %param.14), channel_id=1, source_target_pairs={{0,128},{8,136},{16,144},{24,152},{32,160},{40,168},{48,176},{56,1... | collective-permute-start | bytes 393224 | tf_op jit(solution)/shard_map/ppermute | solution.py:271
  10.5 8.4 %collective-permute-start.1 = (bf16[512,128]{1,0:T(8,128)(2,1)}, bf16[512,128]{1,0:T(8,128)(2,1)S(1)}, u32[]{:S(2)}, u32[]{:S(2)}) collective-permute-start(bf16[512,128]{1,0:T(8,128)(2,1)} %param.14), channel_id=1, source_target_pairs={{0,16},{8,24},{16,0},{24,8},{32,48},{40,56},{48,32},{56,40},{64,80... | collective-permute-start | bytes 393224 | tf_op jit(solution)/shard_map/ppermute | solution.py:271
  11.5 7.8 %collective-permute-start.3 = (bf16[512,128]{1,0:T(8,128)(2,1)}, bf16[512,128]{1,0:T(8,128)(2,1)S(1)}, u32[]{:S(2)}, u32[]{:S(2)}) collective-permute-start(bf16[512,128]{1,0:T(8,128)(2,1)} %param.14), channel_id=1, source_target_pairs={{0,144},{8,152},{16,128},{24,136},{32,176},{40,184},{48,160},{56,1... | collective-permute-start | bytes 393224 | tf_op jit(solution)/shard_map/ppermute | solution.py:271
  14.7 36.6 %copy-start.11 = (s32[6]{0:T(128)}, s32[6]{0:T(128)S(1)}, u32[]{:S(2)}) copy-start(s32[6]{0:T(128)S(1)} %stack.57.place) | copy-start | bytes 76
  19.3 12.5 %copy-start.16 = (bf16[512,128]{1,0:T(8,128)(2,1)S(1)}, bf16[512,128]{1,0:T(8,128)(2,1)}, u32[]{:S(2)}) copy-start(bf16[512,128]{1,0:T(8,128)(2,1)} %param.14) | copy-start | bytes 393220
  19.3 12.8 %collective-permute-start.7 = (bf16[128,512]{1,0:T(8,128)(2,1)S(1)}, bf16[128,512]{1,0:T(8,128)(2,1)S(1)}, u32[]{:S(2)}, u32[]{:S(2)}) collective-permute-start(bf16[128,512]{1,0:T(8,128)(2,1)S(1)} %collective-permute-done), channel_id=1, source_target_pairs={{0,6},{1,7},{2,4},{3,5},{4,2},{5,3},{6,0},{7,1},{8,14},{9,15},{10,... | collective-permute-start | bytes 393224 | tf_op jit(solution)/shard_map/ppermute | solution.py:271
  21.2 10.9 %collective-permute-start.6 = (bf16[128,512]{1,0:T(8,128)(2,1)S(1)}, bf16[128,512]{1,0:T(8,128)(2,1)S(1)}, u32[]{:S(2)}, u32[]{:S(2)}) collective-permute-start(bf16[128,512]{1,0:T(8,128)(2,1)S(1)} %collective-permute-done), channel_id=1, source_target_pairs={{0,4},{1,5},{2,6},{3,7},{4,0},{5,1},{6,2},{7,3},{8,12},{9,13},{10,... | collective-permute-start | bytes 393224 | tf_op jit(solution)/shard_map/ppermute | solution.py:271
  22.3 9.8 %collective-permute-start.5 = (bf16[128,512]{1,0:T(8,128)(2,1)S(1)}, bf16[128,512]{1,0:T(8,128)(2,1)S(1)}, u32[]{:S(2)}, u32[]{:S(2)}) collective-permute-start(bf16[128,512]{1,0:T(8,128)(2,1)S(1)} %collective-permute-done), channel_id=1, source_target_pairs={{0,2},{1,3},{2,0},{3,1},{4,6},{5,7},{6,4},{7,5},{8,10},{9,11},{10,... | collective-permute-start | bytes 393224 | tf_op jit(solution)/shard_map/ppermute | solution.py:271
  23.4 25.0 %all-to-all-start = ((bf16[32,48,128]{2,1,0:T(8,128)(2,1)}), bf16[32,48,128]{2,1,0:T(8,128)(2,1)S(1)}, u32[]{:S(2)}, u32[]{:S(2)}) async-start(bf16[32,48,128]{2,1,0:T(8,128)(2,1)} %bitcast.2), calls=%async_computation | async-start | bytes 786432 | tf_op jit(solution)/shard_map/all_to_all | solution.py:293
  31.9 19.4 %collective-permute-start.4 = (bf16[4,512,128]{2,1,0:T(8,128)(2,1)S(1)}, bf16[4,512,128]{2,1,0:T(8,128)(2,1)S(1)}, u32[]{:S(2)}, u32[]{:S(2)}) collective-permute-start(bf16[4,512,128]{2,1,0:T(8,128)(2,1)S(1)} %pad_maximum_fusion.w_near), channel_id=1, source_target_pairs={{0,8},{8,0},{16,24},{24,16},{32,40},{40,32},{48,56},{56,48},{64,72... | collective-permute-start | bytes 1572872 | tf_op jit(solution)/shard_map/ppermute | solution.py:271
  32.2 1.6 %copy-start = (bf16[2,256,256]{2,1,0:T(8,128)(2,1)S(1)}, bf16[2,256,256]{2,1,0:T(8,128)(2,1)}, u32[]{:S(2)}) copy-start(bf16[2,256,256]{2,1,0:T(8,128)(2,1)} %constant.27.clone.second) | copy-start | bytes 786436
  32.2 1.6 %copy-start.3 = (f32[2,40,128]{2,1,0:T(8,128)S(1)}, f32[2,40,128]{2,1,0:T(8,128)}, u32[]{:S(2)}) copy-start(f32[2,40,128]{2,1,0:T(8,128)} %constant.26.clone.twist) | copy-start | bytes 122884
  32.2 1.5 %copy-start.5 = (bf16[2,80,32]{2,1,0:T(8,128)(2,1)S(1)}, bf16[2,80,32]{2,1,0:T(8,128)(2,1)}, u32[]{:S(2)}) copy-start(bf16[2,80,32]{2,1,0:T(8,128)(2,1)} %constant.25.clone.first) | copy-start | bytes 30724
  32.2 1.5 %copy-start.7 = (f32[16,4096]{1,0:T(8,128)S(1)}, f32[16,4096]{1,0:T(8,128)}, u32[]{:S(2)}) copy-start(f32[16,4096]{1,0:T(8,128)} %filters.1) | copy-start | bytes 786436
  32.3 16.1 %copy-start.8 = (bf16[2,32,80]{2,1,0:T(8,128)(2,1)S(1)}, bf16[2,32,80]{2,1,0:T(8,128)(2,1)}, u32[]{:S(2)}) copy-start(bf16[2,32,80]{2,1,0:T(8,128)(2,1)} %constant.28.clone.last) | copy-start | bytes 30724
  32.3 16.1 %copy-start.9 = (f32[3,3,16]{2,1,0:T(4,128)S(1)}, f32[3,3,16]{2,1,0:T(4,128)}, u32[]{:S(2)}) copy-start(f32[3,3,16]{2,1,0:T(4,128)} %short_w.3) | copy-start | bytes 1732
  32.3 16.1 %copy-start.13 = (f32[16]{0:T(128)S(1)}, f32[16]{0:T(128)}, u32[]{:S(2)}) copy-start(f32[16]{0:T(128)} %skip.3) | copy-start | bytes 196
  32.3 19.0 %collective-permute-start.8 = (bf16[4,128,512]{2,1,0:T(8,128)(2,1)S(1)}, bf16[4,128,512]{2,1,0:T(8,128)(2,1)S(1)}, u32[]{:S(2)}, u32[]{:S(2)}) collective-permute-start(bf16[4,128,512]{2,1,0:T(8,128)(2,1)S(1)} %pad_maximum_fusion.1.g_near), channel_id=1, source_target_pairs={{0,1},{1,0},{2,3},{3,2},{4,5},{5,4},{6,7},{7,6},{8,9},{9,8},{10,11... | collective-permute-start | bytes 1572872 | tf_op jit(solution)/shard_map/ppermute | solution.py:271
  52.8 38.3 %copy-start.12 = (s32[6]{0:T(128)S(1)}, s32[6]{0:T(128)}, u32[]{:S(2)}) copy-start(s32[6]{0:T(128)} %copy-done.11) | copy-start | bytes 76
  91.1 4.6 %copy-start.4 = (f32[2,40,128]{2,1,0:T(8,128)S(1)}, f32[2,40,128]{2,1,0:T(8,128)}, u32[]{:S(2)}) copy-start(f32[2,40,128]{2,1,0:T(8,128)} %constant.26.clone.twist) | copy-start | bytes 122884
  91.1 4.6 %copy-start.6 = (bf16[2,80,32]{2,1,0:T(8,128)(2,1)S(1)}, bf16[2,80,32]{2,1,0:T(8,128)(2,1)}, u32[]{:S(2)}) copy-start(bf16[2,80,32]{2,1,0:T(8,128)(2,1)} %constant.25.clone.first) | copy-start | bytes 30724
  94.2 6.4 %copy-start.1 = (bf16[4,128,512]{2,1,0:T(8,128)(2,1)}, bf16[4,128,512]{2,1,0:T(8,128)(2,1)S(1)}, u32[]{:S(2)}) copy-start(bf16[4,128,512]{2,1,0:T(8,128)(2,1)S(1)} %get-tuple-element.31) | copy-start | bytes 1572868
  94.2 6.4 %copy-start.15 = (bf16[4,512,128]{2,1,0:T(8,128)(2,1)}, bf16[4,512,128]{2,1,0:T(8,128)(2,1)S(1)}, u32[]{:S(2)}) copy-start(bf16[4,512,128]{2,1,0:T(8,128)(2,1)S(1)} %get-tuple-element.41) | copy-start | bytes 1572868
  94.2 1.5 %copy-start.10 = (f32[3,3,16]{2,1,0:T(4,128)S(1)}, f32[3,3,16]{2,1,0:T(4,128)}, u32[]{:S(2)}) copy-start(f32[3,3,16]{2,1,0:T(4,128)} %short_w.3) | copy-start | bytes 1732
  94.2 13.8 %collective-permute-start.9 = (bf16[4,128,512]{2,1,0:T(8,128)(2,1)}, bf16[4,128,512]{2,1,0:T(8,128)(2,1)S(1)}, u32[]{:S(2)}, u32[]{:S(2)}) collective-permute-start(bf16[4,128,512]{2,1,0:T(8,128)(2,1)} %get-tuple-element.32), channel_id=1, source_target_pairs={{0,1},{1,0},{2,3},{3,2},{4,5},{5,4},{6,7},{7,6},{8,9},{9,8},{10,11... | collective-permute-start | bytes 1572872 | tf_op jit(solution)/shard_map/ppermute | solution.py:271
  95.7 0.7 copy-start.14
  100.6 7.4 %copy-start.2 = (bf16[4,128,512]{2,1,0:T(8,128)(2,1)S(1)}, bf16[4,128,512]{2,1,0:T(8,128)(2,1)}, u32[]{:S(2)}) copy-start(bf16[4,128,512]{2,1,0:T(8,128)(2,1)} %copy-done.1) | copy-start | bytes 1572868
  100.6 23.8 %all-to-all-start.2 = ((bf16[32,48,128]{2,1,0:T(8,128)(2,1)}), bf16[32,48,128]{2,1,0:T(8,128)(2,1)S(1)}, u32[]{:S(2)}, u32[]{:S(2)}) async-start(bf16[32,48,128]{2,1,0:T(8,128)(2,1)} %get-tuple-element.38), calls=%async_computation.2 | async-start | bytes 786432 | tf_op jit(solution)/shard_map/all_to_all | solution.py:380
  104.4 8.0 %collective-permute-start.14 = (bf16[4,512,128]{2,1,0:T(8,128)(2,1)}, bf16[4,512,128]{2,1,0:T(8,128)(2,1)S(1)}, u32[]{:S(2)}, u32[]{:S(2)}) collective-permute-start(bf16[4,512,128]{2,1,0:T(8,128)(2,1)} %copy-done.15), channel_id=1, source_target_pairs={{0,8},{8,0},{16,24},{24,16},{32,40},{40,32},{48,56},{56,48},{64,72... | collective-permute-start | bytes 1572872 | tf_op jit(solution)/shard_map/ppermute | solution.py:271
  108.2 6.0 %collective-permute-start.10 = (bf16[128,512]{1,0:T(8,128)(2,1)S(1)}, bf16[128,512]{1,0:T(8,128)(2,1)S(1)}, u32[]{:S(2)}, u32[]{:S(2)}) collective-permute-start(bf16[128,512]{1,0:T(8,128)(2,1)S(1)} %get-tuple-element.49), channel_id=1, source_target_pairs={{0,2},{1,3},{2,0},{3,1},{4,6},{5,7},{6,4},{7,5},{8,10},{9,11},{10,... | collective-permute-start | bytes 393224 | tf_op jit(solution)/shard_map/ppermute | solution.py:271
  108.8 8.8 %collective-permute-start.12 = (bf16[128,512]{1,0:T(8,128)(2,1)S(1)}, bf16[128,512]{1,0:T(8,128)(2,1)S(1)}, u32[]{:S(2)}, u32[]{:S(2)}) collective-permute-start(bf16[128,512]{1,0:T(8,128)(2,1)S(1)} %get-tuple-element.50), channel_id=1, source_target_pairs={{0,6},{1,7},{2,4},{3,5},{4,2},{5,3},{6,0},{7,1},{8,14},{9,15},{10,... | collective-permute-start | bytes 393224 | tf_op jit(solution)/shard_map/ppermute | solution.py:271
  111.1 6.5 %collective-permute-start.11 = (bf16[128,512]{1,0:T(8,128)(2,1)S(1)}, bf16[128,512]{1,0:T(8,128)(2,1)S(1)}, u32[]{:S(2)}, u32[]{:S(2)}) collective-permute-start(bf16[128,512]{1,0:T(8,128)(2,1)S(1)} %get-tuple-element.51), channel_id=1, source_target_pairs={{0,4},{1,5},{2,6},{3,7},{4,0},{5,1},{6,2},{7,3},{8,12},{9,13},{10,... | collective-permute-start | bytes 393224 | tf_op jit(solution)/shard_map/ppermute | solution.py:271
  112.5 8.6 %collective-permute-start.15 = (bf16[512,128]{1,0:T(8,128)(2,1)S(1)}, bf16[512,128]{1,0:T(8,128)(2,1)S(1)}, u32[]{:S(2)}, u32[]{:S(2)}) collective-permute-start(bf16[512,128]{1,0:T(8,128)(2,1)S(1)} %get-tuple-element.46), channel_id=1, source_target_pairs={{0,16},{8,24},{16,0},{24,8},{32,48},{40,56},{48,32},{56,40},{64,80... | collective-permute-start | bytes 393224 | tf_op jit(solution)/shard_map/ppermute | solution.py:271
  112.6 9.8 %collective-permute-start.17 = (bf16[512,128]{1,0:T(8,128)(2,1)S(1)}, bf16[512,128]{1,0:T(8,128)(2,1)S(1)}, u32[]{:S(2)}, u32[]{:S(2)}) collective-permute-start(bf16[512,128]{1,0:T(8,128)(2,1)S(1)} %get-tuple-element.47), channel_id=1, source_target_pairs={{0,144},{8,152},{16,128},{24,136},{32,176},{40,184},{48,160},{56,1... | collective-permute-start | bytes 393224 | tf_op jit(solution)/shard_map/ppermute | solution.py:271
  114.2 9.4 %collective-permute-start.16 = (bf16[512,128]{1,0:T(8,128)(2,1)S(1)}, bf16[512,128]{1,0:T(8,128)(2,1)S(1)}, u32[]{:S(2)}, u32[]{:S(2)}) collective-permute-start(bf16[512,128]{1,0:T(8,128)(2,1)S(1)} %get-tuple-element.48), channel_id=1, source_target_pairs={{0,128},{8,136},{16,144},{24,152},{32,160},{40,168},{48,176},{56,1... | collective-permute-start | bytes 393224 | tf_op jit(solution)/shard_map/ppermute | solution.py:271
  117.7 14.2 %collective-permute-start.13 = (bf16[128,512]{1,0:T(8,128)(2,1)S(1)}, bf16[128,512]{1,0:T(8,128)(2,1)S(1)}, u32[]{:S(2)}, u32[]{:S(2)}) collective-permute-start(bf16[128,512]{1,0:T(8,128)(2,1)S(1)} %fusion.7), channel_id=1, source_target_pairs={{0,0},{1,32},{2,64},{3,96},{4,4},{5,36},{6,68},{7,100},{8,8},{9,40... | collective-permute-start | bytes 393224 | tf_op jit(solution)/shard_map/ppermute | solution.py:281

commit v2 on v1

--- a/solution.py
+++ b/solution.py
@@ -19,7 +19,7 @@
 HALF = 40
 VM = pl.BlockSpec(memory_space=pltpu.VMEM)
 SM = pl.BlockSpec(memory_space=pltpu.SMEM)
-PARAMS = pltpu.CompilerParams(vmem_limit_bytes=48 * 1024 * 1024)
+PARAMS = pltpu.CompilerParams(vmem_limit_bytes=32 * 1024 * 1024)
 
 
 def split(table):
@@ -294,7 +294,6 @@
     near = jnp.stack([tile] + [flip(tile, "tp", 8, m) for m in (2, 4, 6)])
     tiles = [near, flip(near, "tp", 8, 1)]
     w_near = jnp.stack([w_out, *w_got])
-    streams, _ = lax.optimization_barrier((streams, near))
     w_far = flip(w_near, "ctx", 32, 1)
 
     kernel = pl.pallas_call(
@@ -349,16 +348,15 @@
 
     o_sum = o_near.astype(F32) + flip(o_far, "tp", 8, 1).astype(F32)
     o_sent = o_sum.astype(BF16)
-    o_total = o_sum[0]
+    o_total = o_sent[0].astype(F32)
     for k in range(1, 4):
         o_total = o_total + flip(o_sent[k], "tp", 8, 2 * k).astype(F32)
     output = exchange(o_total.astype(BF16))
 
-    d_sum = d_near.astype(F32) + flip(d_far, "ctx", 32, 1).astype(F32)
-    d_sent = d_sum.astype(BF16)
-    d_total = d_sum[0]
+    d_sum = (d_near.astype(F32) + flip(d_far, "ctx", 32, 1).astype(F32)).astype(BF16)
+    d_total = d_sum[0].astype(F32)
     for k, m in ((1, 2), (2, 16), (3, 18)):
-        d_total = d_total + flip(d_sent[k], "ctx", 32, m).astype(F32)
+        d_total = d_total + flip(d_sum[k], "ctx", 32, m).astype(F32)
     grad_w_out = d_total * (SEQ**-0.5)
 
     grads, grad_filters = pl.pallas_call(

time: 133 us -> 133 us (level)
  no operation moved by 1% of the time
where the time goes in v2:
time: 133 us
  starting transfers between devices  44.3 us (33%)
  blocking collectives  38.3 us (29%)
  waiting for transfers between devices  31.3 us (24%)
  Pallas kernels  12.5 us (9%)
  local copies, waits for them, and re-layouts  4.04 us (3%)
    all_to_all x1, blocking collectives, shards(): joint = lax.all_to_all(buffer, 'ctx', 0, 0)  38.3 us
    ppermute x16, starting transfers between devices, flip(): return lax.ppermute(values, axis, [(i, i ^ mask) for i in range(size)])  21.6 us
    all_to_all x1, waiting for transfers between devices, shards(): streams = lax.all_to_all(sent, 'ctx', 0, 0)  13.7 us
    ppermute x2, waiting for transfers between devices, exchange(): return lax.ppermute(values, ('ctx', 'tp'), pairs)  11 us
    ppermute x2, starting transfers between devices, exchange(): return lax.ppermute(values, ('ctx', 'tp'), pairs)  10.5 us
    all_to_all x1, starting transfers between devices, shards(): streams = lax.all_to_all(sent, 'ctx', 0, 0)  8.39 us
    ppermute x16, waiting for transfers between devices, flip(): return lax.ppermute(values, axis, [(i, i ^ mask) for i in range(size)])  6.61 us
    pallas_call x1, Pallas kernels, shards(): pl.pallas_call(rear_kernel, out_shape=[half(SH, 3 * CH, LN), flat(CH, SEQ...  4.21 us
  transfers between devices with their start and end apart: 20, of which 7 were waited for; matrix products, arithmetic and copies ran while one was open for 3% of the time, Pallas kernels for 6%

profile of v2, /device:TPU:42, one launch (start us, length us, event | category | flops | bytes accessed | tf_op | source)
XLA Modules:
  0.0 132.6 jit_solution(8264906261278228677)
XLA Ops:
  0.6 7.2 %collective-permute-start = (bf16[128,512]{1,0:T(8,128)(2,1)}, bf16[128,512]{1,0:T(8,128)(2,1)S(1)}, u32[]{:S(2)}, u32[]{:S(2)}) collective-permute-start(bf16[128,512]{1,0:T(8,128)(2,1)} %param.15), channel_id=1, source_target_pairs={{0,0},{1,32},{2,64},{3,96},{4,4},{5,36},{6,68},{7,100},{8,8},{9,40... | collective-permute-start | bytes 393224 | tf_op jit(solution)/shard_map/ppermute | solution.py:281
  7.8 2.7 %collective-permute-start.2 = (bf16[512,128]{1,0:T(8,128)(2,1)}, bf16[512,128]{1,0:T(8,128)(2,1)S(1)}, u32[]{:S(2)}, u32[]{:S(2)}) collective-permute-start(bf16[512,128]{1,0:T(8,128)(2,1)} %param.14), channel_id=1, source_target_pairs={{0,128},{8,136},{16,144},{24,152},{32,160},{40,168},{48,176},{56,1... | collective-permute-start | bytes 393224 | tf_op jit(solution)/shard_map/ppermute | solution.py:271
  10.5 1.0 collective-permute-start.1
  11.5 1.4 %collective-permute-start.3 = (bf16[512,128]{1,0:T(8,128)(2,1)}, bf16[512,128]{1,0:T(8,128)(2,1)S(1)}, u32[]{:S(2)}, u32[]{:S(2)}) collective-permute-start(bf16[512,128]{1,0:T(8,128)(2,1)} %param.14), channel_id=1, source_target_pairs={{0,144},{8,152},{16,128},{24,136},{32,176},{40,184},{48,160},{56,1... | collective-permute-start | bytes 393224 | tf_op jit(solution)/shard_map/ppermute | solution.py:271
  12.9 1.8 %copy.15 = bf16[3,32,16,128]{3,2,0,1:T(8,128)(2,1)} copy(bf16[3,32,16,128]{3,2,1,0:T(8,128)(2,1)} %bitcast.45) | data formatting | bytes 786432 | tf_op jit(solution)/shard_map/reshape | solution.py:289
  14.7 0.1 stack.57.place
  14.7 4.1 %collective-permute-done = bf16[128,512]{1,0:T(8,128)(2,1)S(1)} collective-permute-done((bf16[128,512]{1,0:T(8,128)(2,1)}, bf16[128,512]{1,0:T(8,128)(2,1)S(1)}, u32[]{:S(2)}, u32[]{:S(2)}) %collective-permute-start) | collective-permute-done | bytes 131104 | tf_op jit(solution)/shard_map/ppermute | solution.py:281
  18.9 0.4 collective-permute-done.3
  19.3 1.9 %collective-permute-start.7 = (bf16[128,512]{1,0:T(8,128)(2,1)S(1)}, bf16[128,512]{1,0:T(8,128)(2,1)S(1)}, u32[]{:S(2)}, u32[]{:S(2)}) collective-permute-start(bf16[128,512]{1,0:T(8,128)(2,1)S(1)} %collective-permute-done), channel_id=1, source_target_pairs={{0,6},{1,7},{2,4},{3,5},{4,2},{5,3},{6,0},{7,1},{8,14},{9,15},{10,... | collective-permute-start | bytes 393224 | tf_op jit(solution)/shard_map/ppermute | solution.py:271
  21.2 1.1 collective-permute-start.6
  22.3 1.1 collective-permute-start.5
  23.4 8.4 %all-to-all-start = ((bf16[32,48,128]{2,1,0:T(8,128)(2,1)}), bf16[32,48,128]{2,1,0:T(8,128)(2,1)S(1)}, u32[]{:S(2)}, u32[]{:S(2)}) async-start(bf16[32,48,128]{2,1,0:T(8,128)(2,1)} %bitcast.2), calls=%async_computation | async-start | bytes 786432 | tf_op jit(solution)/shard_map/all_to_all | solution.py:293
  31.8 0.1 pad_maximum_fusion.w_near
  31.9 0.2 collective-permute-start.4
  32.2 0.0 copy-start
  32.2 0.0 copy-start.3
  32.2 0.0 copy-start.5
  32.2 0.0 copy-start.7
  32.2 0.1 pad_maximum_fusion.1.g_near
  32.3 0.0 copy-start.8
  32.3 1.4 %collective-permute-start.8 = (bf16[4,128,512]{2,1,0:T(8,128)(2,1)S(1)}, bf16[4,128,512]{2,1,0:T(8,128)(2,1)S(1)}, u32[]{:S(2)}, u32[]{:S(2)}) collective-permute-start(bf16[4,128,512]{2,1,0:T(8,128)(2,1)S(1)} %pad_maximum_fusion.1.g_near), channel_id=1, source_target_pairs={{0,1},{1,0},{2,3},{3,2},{4,5},{5,4},{6,7},{7,6},{8,9},{9,8},{10,11... | collective-permute-start | bytes 1572872 | tf_op jit(solution)/shard_map/ppermute | solution.py:271
  33.7 0.9 filter_spectrum.1.kernel
  34.6 13.7 %all-to-all-done.streams = bf16[32,48,128]{2,1,0:T(8,128)(2,1)S(1)} async-done(((bf16[32,48,128]{2,1,0:T(8,128)(2,1)}), bf16[32,48,128]{2,1,0:T(8,128)(2,1)S(1)}, u32[]{:S(2)}, u32[]{:S(2)}) %all-to-all-start) | async-done | bytes 393248 | tf_op jit(solution)/shard_map/all_to_all | solution.py:293
  48.4 2.9 %front.1 = (bf16[32,32,512]{2,1,0:T(8,128)(2,1)S(1)}, f32[32,2048]{1,0:T(8,128)S(1)}, f32[32,2048]{1,0:T(8,128)S(1)}, f32[32,2048]{1,0:T(8,128)S(1)}, f32[32,2048]{1,0:T(8,128)S(1)}, /*index=5*/f32[640,256]{1,0:T(8,128)S(1)}) custom-call(bf16[32,48,128]{2,1,0:T(8,128)(2,1)S(1)} %all-to-all-done.streams, f32[3,3,16]{2,1,0:T(4,128)S(1)} %copy-done.9, ...), custom_call_target="tpu_custom_call" | custom-call | tf_op jit(solution)/shard_map/front/pallas_call | solution.py:309
  51.3 1.5 %mixed_grad.1 = bf16[32,32,512]{2,1,0:T(8,128)(2,1)S(1)} custom-call(s32[6]{0:T(128)S(1)} %stack.57.place, bf16[4,512,128]{2,1,0:T(8,128)(2,1)S(1)} %pad_maximum_fusion.w_near, bf16[4,512,128]{2,1,0:T(8,128)(2,1)S(1)} %collective-permute-done.4.w_far, bf16[4,128,512]{2,1,0:T(8,128)(2,1)S(1)} %pad_maximum_fusion.1.g_near, ...), custom_call_target="tpu_custom_call", output_to_operand_aliasing={{}: (5, {})} | custom-call | tf_op jit(solution)/shard_map/mixed_grad/pallas_call | solution.py:324
  52.8 38.3 %all_to_all.15.mixed.upstream = bf16[32,32,512]{2,1,0:T(8,128)(2,1)S(1)} all-to-all(bf16[32,32,512]{2,1,0:T(8,128)(2,1)S(1)} %mixed_grad.1), channel_id=1, replica_groups=mesh['ctx'=32,'tp'=8] {'ctx'}, dimensions={0} | all-to-all | bytes 2097152 | tf_op jit(solution)/shard_map/all_to_all | solution.py:336
  91.1 3.0 %projections.1 = (bf16[4,128,512]{2,1,0:T(8,128)(2,1)S(1)}, bf16[4,128,512]{2,1,0:T(8,128)(2,1)}, bf16[4,512,128]{2,1,0:T(8,128)(2,1)S(1)}, bf16[4,512,128]{2,1,0:T(8,128)(2,1)}) custom-call(s32[6]{0:T(128)S(1)} %copy-done.12, bf16[32,32,512]{2,1,0:T(8,128)(2,1)S(1)} %all_to_all.15.mixed.upstream, bf16[4,512,128]{2,1,0:T(8,128)(2,1)S(1)} %pad_maximum_fusion.w_near, ...), custom_call_target="tpu_custom_call" | custom-call | tf_op jit(solution)/shard_map/projections/pallas_call | solution.py:338
  94.2 1.5 %collective-permute-start.9 = (bf16[4,128,512]{2,1,0:T(8,128)(2,1)}, bf16[4,128,512]{2,1,0:T(8,128)(2,1)S(1)}, u32[]{:S(2)}, u32[]{:S(2)}) collective-permute-start(bf16[4,128,512]{2,1,0:T(8,128)(2,1)} %get-tuple-element.30), channel_id=1, source_target_pairs={{0,1},{1,0},{2,3},{3,2},{4,5},{5,4},{6,7},{7,6},{8,9},{9,8},{10,11... | collective-permute-start | bytes 1572872 | tf_op jit(solution)/shard_map/ppermute | solution.py:271
  95.7 0.6 copy-done.14
  96.3 4.2 %rear.1 = (bf16[32,48,128]{2,1,0:T(8,128)(2,1)}, f32[16,4096]{1,0:T(8,128)}) custom-call(bf16[32,32,512]{2,1,0:T(8,128)(2,1)S(1)} %all_to_all.15.mixed.upstream, f32[3,3,16]{2,1,0:T(4,128)S(1)} %copy-done.10, f32[16]{0:T(128)S(1)} %copy-done.14, f32[640,256]{1,0:T(8,128)S(1)} %filter_spectrum.1.kernel, f32[640,256]{1,0:T(8,128)S(1)} %get-tuple-element.31.spectrum, ...), custom_call_target="tpu_custom_call" | custom-call | tf_op jit(solution)/shard_map/rear/pallas_call | solution.py:362
  100.6 3.8 %all-to-all-start.2 = ((bf16[32,48,128]{2,1,0:T(8,128)(2,1)}), bf16[32,48,128]{2,1,0:T(8,128)(2,1)S(1)}, u32[]{:S(2)}, u32[]{:S(2)}) async-start(bf16[32,48,128]{2,1,0:T(8,128)(2,1)} %get-tuple-element.36), calls=%async_computation.2 | async-start | bytes 786432 | tf_op jit(solution)/shard_map/all_to_all | solution.py:378
  104.4 3.6 %collective-permute-done.9 = bf16[4,128,512]{2,1,0:T(8,128)(2,1)S(1)} collective-permute-done((bf16[4,128,512]{2,1,0:T(8,128)(2,1)}, bf16[4,128,512]{2,1,0:T(8,128)(2,1)S(1)}, u32[]{:S(2)}, u32[]{:S(2)}) %collective-permute-start.9) | collective-permute-done | bytes 524320 | tf_op jit(solution)/shard_map/ppermute | solution.py:271
  107.9 0.1 add_convert_fusion.1
  108.1 0.6 collective-permute-start.10
  108.7 2.3 %collective-permute-start.12 = (bf16[128,512]{1,0:T(8,128)(2,1)S(1)}, bf16[128,512]{1,0:T(8,128)(2,1)S(1)}, u32[]{:S(2)}, u32[]{:S(2)}) collective-permute-start(bf16[128,512]{1,0:T(8,128)(2,1)S(1)} %get-tuple-element.44), channel_id=1, source_target_pairs={{0,6},{1,7},{2,4},{3,5},{4,2},{5,3},{6,0},{7,1},{8,14},{9,15},{10,... | collective-permute-start | bytes 393224 | tf_op jit(solution)/shard_map/ppermute | solution.py:271
  111.0 1.3 collective-permute-start.11
  112.3 0.1 add_convert_fusion
  112.5 0.1 collective-permute-start.15
  112.6 1.5 %collective-permute-start.17 = (bf16[512,128]{1,0:T(8,128)(2,1)S(1)}, bf16[512,128]{1,0:T(8,128)(2,1)S(1)}, u32[]{:S(2)}, u32[]{:S(2)}) collective-permute-start(bf16[512,128]{1,0:T(8,128)(2,1)S(1)} %get-tuple-element.41), channel_id=1, source_target_pairs={{0,144},{8,152},{16,128},{24,136},{32,176},{40,184},{48,160},{56,1... | collective-permute-start | bytes 393224 | tf_op jit(solution)/shard_map/ppermute | solution.py:271
  114.1 3.5 %collective-permute-start.16 = (bf16[512,128]{1,0:T(8,128)(2,1)S(1)}, bf16[512,128]{1,0:T(8,128)(2,1)S(1)}, u32[]{:S(2)}, u32[]{:S(2)}) collective-permute-start(bf16[512,128]{1,0:T(8,128)(2,1)S(1)} %get-tuple-element.42), channel_id=1, source_target_pairs={{0,128},{8,136},{16,144},{24,152},{32,160},{40,168},{48,176},{56,1... | collective-permute-start | bytes 393224 | tf_op jit(solution)/shard_map/ppermute | solution.py:271
  117.6 0.1 fusion.5
  117.6 3.3 %collective-permute-start.13 = (bf16[128,512]{1,0:T(8,128)(2,1)S(1)}, bf16[128,512]{1,0:T(8,128)(2,1)S(1)}, u32[]{:S(2)}, u32[]{:S(2)}) collective-permute-start(bf16[128,512]{1,0:T(8,128)(2,1)S(1)} %fusion.5), channel_id=1, source_target_pairs={{0,0},{1,32},{2,64},{3,96},{4,4},{5,36},{6,68},{7,100},{8,8},{9,40... | collective-permute-start | bytes 393224 | tf_op jit(solution)/shard_map/ppermute | solution.py:281
  121.0 1.5 %collective-permute-done.17 = bf16[512,128]{1,0:T(8,128)(2,1)S(1)} collective-permute-done((bf16[512,128]{1,0:T(8,128)(2,1)S(1)}, bf16[512,128]{1,0:T(8,128)(2,1)S(1)}, u32[]{:S(2)}, u32[]{:S(2)}) %collective-permute-start.17) | collective-permute-done | bytes 131104 | tf_op jit(solution)/shard_map/ppermute | solution.py:271
  122.5 1.1 collective-permute-done.16
  123.6 0.8 fusion.2
  124.4 0.8 copy.16
  125.1 6.8 %collective-permute-done.13 = bf16[128,512]{1,0:T(8,128)(2,1)S(1)} collective-permute-done((bf16[128,512]{1,0:T(8,128)(2,1)S(1)}, bf16[128,512]{1,0:T(8,128)(2,1)S(1)}, u32[]{:S(2)}, u32[]{:S(2)}) %collective-permute-start.13) | collective-permute-done | bytes 131104 | tf_op jit(solution)/shard_map/ppermute | solution.py:281
  132.0 0.7 copy.19
  (42 shorter events, 0.2 us)
Async XLA Ops:
  0.6 18.3 %collective-permute-start = (bf16[128,512]{1,0:T(8,128)(2,1)}, bf16[128,512]{1,0:T(8,128)(2,1)S(1)}, u32[]{:S(2)}, u32[]{:S(2)}) collective-permute-start(bf16[128,512]{1,0:T(8,128)(2,1)} %param.15), channel_id=1, source_target_pairs={{0,0},{1,32},{2,64},{3,96},{4,4},{5,36},{6,68},{7,100},{8,8},{9,40... | collective-permute-start | bytes 393224 | tf_op jit(solution)/shard_map/ppermute | solution.py:281
  7.8 11.1 %collective-permute-start.2 = (bf16[512,128]{1,0:T(8,128)(2,1)}, bf16[512,128]{1,0:T(8,128)(2,1)S(1)}, u32[]{:S(2)}, u32[]{:S(2)}) collective-permute-start(bf16[512,128]{1,0:T(8,128)(2,1)} %param.14), channel_id=1, source_target_pairs={{0,128},{8,136},{16,144},{24,152},{32,160},{40,168},{48,176},{56,1... | collective-permute-start | bytes 393224 | tf_op jit(solution)/shard_map/ppermute | solution.py:271
  10.5 8.4 %collective-permute-start.1 = (bf16[512,128]{1,0:T(8,128)(2,1)}, bf16[512,128]{1,0:T(8,128)(2,1)S(1)}, u32[]{:S(2)}, u32[]{:S(2)}) collective-permute-start(bf16[512,128]{1,0:T(8,128)(2,1)} %param.14), channel_id=1, source_target_pairs={{0,16},{8,24},{16,0},{24,8},{32,48},{40,56},{48,32},{56,40},{64,80... | collective-permute-start | bytes 393224 | tf_op jit(solution)/shard_map/ppermute | solution.py:271
  11.5 7.8 %collective-permute-start.3 = (bf16[512,128]{1,0:T(8,128)(2,1)}, bf16[512,128]{1,0:T(8,128)(2,1)S(1)}, u32[]{:S(2)}, u32[]{:S(2)}) collective-permute-start(bf16[512,128]{1,0:T(8,128)(2,1)} %param.14), channel_id=1, source_target_pairs={{0,144},{8,152},{16,128},{24,136},{32,176},{40,184},{48,160},{56,1... | collective-permute-start | bytes 393224 | tf_op jit(solution)/shard_map/ppermute | solution.py:271
  14.7 36.6 %copy-start.11 = (s32[6]{0:T(128)}, s32[6]{0:T(128)S(1)}, u32[]{:S(2)}) copy-start(s32[6]{0:T(128)S(1)} %stack.57.place) | copy-start | bytes 76
  19.3 12.5 %copy-start.15 = (bf16[512,128]{1,0:T(8,128)(2,1)S(1)}, bf16[512,128]{1,0:T(8,128)(2,1)}, u32[]{:S(2)}) copy-start(bf16[512,128]{1,0:T(8,128)(2,1)} %param.14) | copy-start | bytes 393220
  19.3 12.8 %collective-permute-start.7 = (bf16[128,512]{1,0:T(8,128)(2,1)S(1)}, bf16[128,512]{1,0:T(8,128)(2,1)S(1)}, u32[]{:S(2)}, u32[]{:S(2)}) collective-permute-start(bf16[128,512]{1,0:T(8,128)(2,1)S(1)} %collective-permute-done), channel_id=1, source_target_pairs={{0,6},{1,7},{2,4},{3,5},{4,2},{5,3},{6,0},{7,1},{8,14},{9,15},{10,... | collective-permute-start | bytes 393224 | tf_op jit(solution)/shard_map/ppermute | solution.py:271
  21.2 10.9 %collective-permute-start.6 = (bf16[128,512]{1,0:T(8,128)(2,1)S(1)}, bf16[128,512]{1,0:T(8,128)(2,1)S(1)}, u32[]{:S(2)}, u32[]{:S(2)}) collective-permute-start(bf16[128,512]{1,0:T(8,128)(2,1)S(1)} %collective-permute-done), channel_id=1, source_target_pairs={{0,4},{1,5},{2,6},{3,7},{4,0},{5,1},{6,2},{7,3},{8,12},{9,13},{10,... | collective-permute-start | bytes 393224 | tf_op jit(solution)/shard_map/ppermute | solution.py:271
  22.3 9.8 %collective-permute-start.5 = (bf16[128,512]{1,0:T(8,128)(2,1)S(1)}, bf16[128,512]{1,0:T(8,128)(2,1)S(1)}, u32[]{:S(2)}, u32[]{:S(2)}) collective-permute-start(bf16[128,512]{1,0:T(8,128)(2,1)S(1)} %collective-permute-done), channel_id=1, source_target_pairs={{0,2},{1,3},{2,0},{3,1},{4,6},{5,7},{6,4},{7,5},{8,10},{9,11},{10,... | collective-permute-start | bytes 393224 | tf_op jit(solution)/shard_map/ppermute | solution.py:271
  23.4 25.0 %all-to-all-start = ((bf16[32,48,128]{2,1,0:T(8,128)(2,1)}), bf16[32,48,128]{2,1,0:T(8,128)(2,1)S(1)}, u32[]{:S(2)}, u32[]{:S(2)}) async-start(bf16[32,48,128]{2,1,0:T(8,128)(2,1)} %bitcast.2), calls=%async_computation | async-start | bytes 786432 | tf_op jit(solution)/shard_map/all_to_all | solution.py:293
  31.9 19.4 %collective-permute-start.4 = (bf16[4,512,128]{2,1,0:T(8,128)(2,1)S(1)}, bf16[4,512,128]{2,1,0:T(8,128)(2,1)S(1)}, u32[]{:S(2)}, u32[]{:S(2)}) collective-permute-start(bf16[4,512,128]{2,1,0:T(8,128)(2,1)S(1)} %pad_maximum_fusion.w_near), channel_id=1, source_target_pairs={{0,8},{8,0},{16,24},{24,16},{32,40},{40,32},{48,56},{56,48},{64,72... | collective-permute-start | bytes 1572872 | tf_op jit(solution)/shard_map/ppermute | solution.py:271
  32.2 1.6 %copy-start = (bf16[2,256,256]{2,1,0:T(8,128)(2,1)S(1)}, bf16[2,256,256]{2,1,0:T(8,128)(2,1)}, u32[]{:S(2)}) copy-start(bf16[2,256,256]{2,1,0:T(8,128)(2,1)} %constant.27.clone.second) | copy-start | bytes 786436
  32.2 1.6 %copy-start.3 = (f32[2,40,128]{2,1,0:T(8,128)S(1)}, f32[2,40,128]{2,1,0:T(8,128)}, u32[]{:S(2)}) copy-start(f32[2,40,128]{2,1,0:T(8,128)} %constant.26.clone.twist) | copy-start | bytes 122884
  32.2 1.5 %copy-start.5 = (bf16[2,80,32]{2,1,0:T(8,128)(2,1)S(1)}, bf16[2,80,32]{2,1,0:T(8,128)(2,1)}, u32[]{:S(2)}) copy-start(bf16[2,80,32]{2,1,0:T(8,128)(2,1)} %constant.25.clone.first) | copy-start | bytes 30724
  32.2 1.5 %copy-start.7 = (f32[16,4096]{1,0:T(8,128)S(1)}, f32[16,4096]{1,0:T(8,128)}, u32[]{:S(2)}) copy-start(f32[16,4096]{1,0:T(8,128)} %filters.1) | copy-start | bytes 786436
  32.3 16.1 %copy-start.8 = (bf16[2,32,80]{2,1,0:T(8,128)(2,1)S(1)}, bf16[2,32,80]{2,1,0:T(8,128)(2,1)}, u32[]{:S(2)}) copy-start(bf16[2,32,80]{2,1,0:T(8,128)(2,1)} %constant.28.clone.last) | copy-start | bytes 30724
  32.3 16.1 %copy-start.9 = (f32[3,3,16]{2,1,0:T(4,128)S(1)}, f32[3,3,16]{2,1,0:T(4,128)}, u32[]{:S(2)}) copy-start(f32[3,3,16]{2,1,0:T(4,128)} %short_w.3) | copy-start | bytes 1732
  32.3 16.1 %copy-start.13 = (f32[16]{0:T(128)S(1)}, f32[16]{0:T(128)}, u32[]{:S(2)}) copy-start(f32[16]{0:T(128)} %skip.3) | copy-start | bytes 196
  32.3 19.0 %collective-permute-start.8 = (bf16[4,128,512]{2,1,0:T(8,128)(2,1)S(1)}, bf16[4,128,512]{2,1,0:T(8,128)(2,1)S(1)}, u32[]{:S(2)}, u32[]{:S(2)}) collective-permute-start(bf16[4,128,512]{2,1,0:T(8,128)(2,1)S(1)} %pad_maximum_fusion.1.g_near), channel_id=1, source_target_pairs={{0,1},{1,0},{2,3},{3,2},{4,5},{5,4},{6,7},{7,6},{8,9},{9,8},{10,11... | collective-permute-start | bytes 1572872 | tf_op jit(solution)/shard_map/ppermute | solution.py:271
  52.8 38.3 %copy-start.12 = (s32[6]{0:T(128)S(1)}, s32[6]{0:T(128)}, u32[]{:S(2)}) copy-start(s32[6]{0:T(128)} %copy-done.11) | copy-start | bytes 76
  91.1 4.6 %copy-start.4 = (f32[2,40,128]{2,1,0:T(8,128)S(1)}, f32[2,40,128]{2,1,0:T(8,128)}, u32[]{:S(2)}) copy-start(f32[2,40,128]{2,1,0:T(8,128)} %constant.26.clone.twist) | copy-start | bytes 122884
  91.1 4.6 %copy-start.6 = (bf16[2,80,32]{2,1,0:T(8,128)(2,1)S(1)}, bf16[2,80,32]{2,1,0:T(8,128)(2,1)}, u32[]{:S(2)}) copy-start(bf16[2,80,32]{2,1,0:T(8,128)(2,1)} %constant.25.clone.first) | copy-start | bytes 30724
  94.1 6.4 %copy-start.1 = (bf16[4,128,512]{2,1,0:T(8,128)(2,1)}, bf16[4,128,512]{2,1,0:T(8,128)(2,1)S(1)}, u32[]{:S(2)}) copy-start(bf16[4,128,512]{2,1,0:T(8,128)(2,1)S(1)} %get-tuple-element.29) | copy-start | bytes 1572868
  94.2 1.6 %copy-start.10 = (f32[3,3,16]{2,1,0:T(4,128)S(1)}, f32[3,3,16]{2,1,0:T(4,128)}, u32[]{:S(2)}) copy-start(f32[3,3,16]{2,1,0:T(4,128)} %short_w.3) | copy-start | bytes 1732
  94.2 13.8 %collective-permute-start.9 = (bf16[4,128,512]{2,1,0:T(8,128)(2,1)}, bf16[4,128,512]{2,1,0:T(8,128)(2,1)S(1)}, u32[]{:S(2)}, u32[]{:S(2)}) collective-permute-start(bf16[4,128,512]{2,1,0:T(8,128)(2,1)} %get-tuple-element.30), channel_id=1, source_target_pairs={{0,1},{1,0},{2,3},{3,2},{4,5},{5,4},{6,7},{7,6},{8,9},{9,8},{10,11... | collective-permute-start | bytes 1572872 | tf_op jit(solution)/shard_map/ppermute | solution.py:271
  95.7 16.6 %collective-permute-start.14 = (bf16[4,512,128]{2,1,0:T(8,128)(2,1)}, bf16[4,512,128]{2,1,0:T(8,128)(2,1)S(1)}, u32[]{:S(2)}, u32[]{:S(2)}) collective-permute-start(bf16[4,512,128]{2,1,0:T(8,128)(2,1)} %get-tuple-element.39), channel_id=1, source_target_pairs={{0,8},{8,0},{16,24},{24,16},{32,40},{40,32},{48,56},{56,48},{64,72... | collective-permute-start | bytes 1572872 | tf_op jit(solution)/shard_map/ppermute | solution.py:271
  95.7 0.7 copy-start.14
  100.6 7.4 %copy-start.2 = (bf16[4,128,512]{2,1,0:T(8,128)(2,1)S(1)}, bf16[4,128,512]{2,1,0:T(8,128)(2,1)}, u32[]{:S(2)}) copy-start(bf16[4,128,512]{2,1,0:T(8,128)(2,1)} %copy-done.1) | copy-start | bytes 1572868
  100.6 23.8 %all-to-all-start.2 = ((bf16[32,48,128]{2,1,0:T(8,128)(2,1)}), bf16[32,48,128]{2,1,0:T(8,128)(2,1)S(1)}, u32[]{:S(2)}, u32[]{:S(2)}) async-start(bf16[32,48,128]{2,1,0:T(8,128)(2,1)} %get-tuple-element.36), calls=%async_computation.2 | async-start | bytes 786432 | tf_op jit(solution)/shard_map/all_to_all | solution.py:378
  108.1 6.0 %collective-permute-start.10 = (bf16[128,512]{1,0:T(8,128)(2,1)S(1)}, bf16[128,512]{1,0:T(8,128)(2,1)S(1)}, u32[]{:S(2)}, u32[]{:S(2)}) collective-permute-start(bf16[128,512]{1,0:T(8,128)(2,1)S(1)} %get-tuple-element.43), channel_id=1, source_target_pairs={{0,2},{1,3},{2,0},{3,1},{4,6},{5,7},{6,4},{7,5},{8,10},{9,11},{10,... | collective-permute-start | bytes 393224 | tf_op jit(solution)/shard_map/ppermute | solution.py:271
  108.7 8.8 %collective-permute-start.12 = (bf16[128,512]{1,0:T(8,128)(2,1)S(1)}, bf16[128,512]{1,0:T(8,128)(2,1)S(1)}, u32[]{:S(2)}, u32[]{:S(2)}) collective-permute-start(bf16[128,512]{1,0:T(8,128)(2,1)S(1)} %get-tuple-element.44), channel_id=1, source_target_pairs={{0,6},{1,7},{2,4},{3,5},{4,2},{5,3},{6,0},{7,1},{8,14},{9,15},{10,... | collective-permute-start | bytes 393224 | tf_op jit(solution)/shard_map/ppermute | solution.py:271
  111.0 6.5 %collective-permute-start.11 = (bf16[128,512]{1,0:T(8,128)(2,1)S(1)}, bf16[128,512]{1,0:T(8,128)(2,1)S(1)}, u32[]{:S(2)}, u32[]{:S(2)}) collective-permute-start(bf16[128,512]{1,0:T(8,128)(2,1)S(1)} %get-tuple-element.45), channel_id=1, source_target_pairs={{0,4},{1,5},{2,6},{3,7},{4,0},{5,1},{6,2},{7,3},{8,12},{9,13},{10,... | collective-permute-start | bytes 393224 | tf_op jit(solution)/shard_map/ppermute | solution.py:271
  112.5 8.5 %collective-permute-start.15 = (bf16[512,128]{1,0:T(8,128)(2,1)S(1)}, bf16[512,128]{1,0:T(8,128)(2,1)S(1)}, u32[]{:S(2)}, u32[]{:S(2)}) collective-permute-start(bf16[512,128]{1,0:T(8,128)(2,1)S(1)} %get-tuple-element.40), channel_id=1, source_target_pairs={{0,16},{8,24},{16,0},{24,8},{32,48},{40,56},{48,32},{56,40},{64,80... | collective-permute-start | bytes 393224 | tf_op jit(solution)/shard_map/ppermute | solution.py:271
  112.6 9.9 %collective-permute-start.17 = (bf16[512,128]{1,0:T(8,128)(2,1)S(1)}, bf16[512,128]{1,0:T(8,128)(2,1)S(1)}, u32[]{:S(2)}, u32[]{:S(2)}) collective-permute-start(bf16[512,128]{1,0:T(8,128)(2,1)S(1)} %get-tuple-element.41), channel_id=1, source_target_pairs={{0,144},{8,152},{16,128},{24,136},{32,176},{40,184},{48,160},{56,1... | collective-permute-start | bytes 393224 | tf_op jit(solution)/shard_map/ppermute | solution.py:271
  114.1 9.5 %collective-permute-start.16 = (bf16[512,128]{1,0:T(8,128)(2,1)S(1)}, bf16[512,128]{1,0:T(8,128)(2,1)S(1)}, u32[]{:S(2)}, u32[]{:S(2)}) collective-permute-start(bf16[512,128]{1,0:T(8,128)(2,1)S(1)} %get-tuple-element.42), channel_id=1, source_target_pairs={{0,128},{8,136},{16,144},{24,152},{32,160},{40,168},{48,176},{56,1... | collective-permute-start | bytes 393224 | tf_op jit(solution)/shard_map/ppermute | solution.py:271
  117.6 14.3 %collective-permute-start.13 = (bf16[128,512]{1,0:T(8,128)(2,1)S(1)}, bf16[128,512]{1,0:T(8,128)(2,1)S(1)}, u32[]{:S(2)}, u32[]{:S(2)}) collective-permute-start(bf16[128,512]{1,0:T(8,128)(2,1)S(1)} %fusion.5), channel_id=1, source_target_pairs={{0,0},{1,32},{2,64},{3,96},{4,4},{5,36},{6,68},{7,100},{8,8},{9,40... | collective-permute-start | bytes 393224 | tf_op jit(solution)/shard_map/ppermute | solution.py:281

commit v3 on v1

--- a/solution.py
+++ b/solution.py
@@ -19,7 +19,7 @@
 HALF = 40
 VM = pl.BlockSpec(memory_space=pltpu.VMEM)
 SM = pl.BlockSpec(memory_space=pltpu.SMEM)
-PARAMS = pltpu.CompilerParams(vmem_limit_bytes=48 * 1024 * 1024)
+PARAMS = pltpu.CompilerParams(vmem_limit_bytes=32 * 1024 * 1024)
 
 
 def split(table):

time: 133 us -> 133 us (level)
  no operation moved by 1% of the time
where the time goes in v3:
time: 133 us
  starting transfers between devices  44.5 us (33%)
  blocking collectives  38.3 us (29%)
  waiting for transfers between devices  31 us (23%)
  Pallas kernels  12.5 us (9%)
  local copies, waits for them, and re-layouts  4.06 us (3%)
    all_to_all x1, blocking collectives, shards(): joint = lax.all_to_all(buffer, 'ctx', 0, 0)  38.3 us
    ppermute x16, starting transfers between devices, flip(): return lax.ppermute(values, axis, [(i, i ^ mask) for i in range(size)])  21.7 us
    all_to_all x1, waiting for transfers between devices, shards(): streams = lax.all_to_all(sent, 'ctx', 0, 0)  13.7 us
    ppermute x2, waiting for transfers between devices, exchange(): return lax.ppermute(values, ('ctx', 'tp'), pairs)  11 us
    ppermute x2, starting transfers between devices, exchange(): return lax.ppermute(values, ('ctx', 'tp'), pairs)  10.6 us
    all_to_all x1, starting transfers between devices, shards(): streams = lax.all_to_all(sent, 'ctx', 0, 0)  8.39 us
    ppermute x16, waiting for transfers between devices, flip(): return lax.ppermute(values, axis, [(i, i ^ mask) for i in range(size)])  6.33 us
    pallas_call x1, Pallas kernels, shards(): pl.pallas_call(rear_kernel, out_shape=[half(SH, 3 * CH, LN), flat(CH, SEQ...  4.21 us
  transfers between devices with their start and end apart: 20, of which 7 were waited for; matrix products, arithmetic and copies ran while one was open for 3% of the time, Pallas kernels for 6%

profile of v3, /device:TPU:42, one launch (start us, length us, event | category | flops | bytes accessed | tf_op | source)
XLA Modules:
  0.0 132.6 jit_solution(3618752131898355253)
XLA Ops:
  0.6 7.2 %collective-permute-start = (bf16[128,512]{1,0:T(8,128)(2,1)}, bf16[128,512]{1,0:T(8,128)(2,1)S(1)}, u32[]{:S(2)}, u32[]{:S(2)}) collective-permute-start(bf16[128,512]{1,0:T(8,128)(2,1)} %param.15), channel_id=1, source_target_pairs={{0,0},{1,32},{2,64},{3,96},{4,4},{5,36},{6,68},{7,100},{8,8},{9,40... | collective-permute-start | bytes 393224 | tf_op jit(solution)/shard_map/ppermute | solution.py:281
  7.8 2.7 %collective-permute-start.2 = (bf16[512,128]{1,0:T(8,128)(2,1)}, bf16[512,128]{1,0:T(8,128)(2,1)S(1)}, u32[]{:S(2)}, u32[]{:S(2)}) collective-permute-start(bf16[512,128]{1,0:T(8,128)(2,1)} %param.14), channel_id=1, source_target_pairs={{0,128},{8,136},{16,144},{24,152},{32,160},{40,168},{48,176},{56,1... | collective-permute-start | bytes 393224 | tf_op jit(solution)/shard_map/ppermute | solution.py:271
  10.5 1.0 collective-permute-start.1
  11.5 1.4 %collective-permute-start.3 = (bf16[512,128]{1,0:T(8,128)(2,1)}, bf16[512,128]{1,0:T(8,128)(2,1)S(1)}, u32[]{:S(2)}, u32[]{:S(2)}) collective-permute-start(bf16[512,128]{1,0:T(8,128)(2,1)} %param.14), channel_id=1, source_target_pairs={{0,144},{8,152},{16,128},{24,136},{32,176},{40,184},{48,160},{56,1... | collective-permute-start | bytes 393224 | tf_op jit(solution)/shard_map/ppermute | solution.py:271
  12.9 1.8 %copy.15 = bf16[3,32,16,128]{3,2,0,1:T(8,128)(2,1)} copy(bf16[3,32,16,128]{3,2,1,0:T(8,128)(2,1)} %bitcast.55) | data formatting | bytes 786432 | tf_op jit(solution)/shard_map/reshape | solution.py:289
  14.7 0.1 stack.57.place
  14.7 4.1 %collective-permute-done = bf16[128,512]{1,0:T(8,128)(2,1)S(1)} collective-permute-done((bf16[128,512]{1,0:T(8,128)(2,1)}, bf16[128,512]{1,0:T(8,128)(2,1)S(1)}, u32[]{:S(2)}, u32[]{:S(2)}) %collective-permute-start) | collective-permute-done | bytes 131104 | tf_op jit(solution)/shard_map/ppermute | solution.py:281
  18.9 0.4 collective-permute-done.3
  19.3 1.9 %collective-permute-start.7 = (bf16[128,512]{1,0:T(8,128)(2,1)S(1)}, bf16[128,512]{1,0:T(8,128)(2,1)S(1)}, u32[]{:S(2)}, u32[]{:S(2)}) collective-permute-start(bf16[128,512]{1,0:T(8,128)(2,1)S(1)} %collective-permute-done), channel_id=1, source_target_pairs={{0,6},{1,7},{2,4},{3,5},{4,2},{5,3},{6,0},{7,1},{8,14},{9,15},{10,... | collective-permute-start | bytes 393224 | tf_op jit(solution)/shard_map/ppermute | solution.py:271
  21.2 1.1 collective-permute-start.6
  22.3 1.1 collective-permute-start.5
  23.4 8.4 %all-to-all-start = ((bf16[32,48,128]{2,1,0:T(8,128)(2,1)}), bf16[32,48,128]{2,1,0:T(8,128)(2,1)S(1)}, u32[]{:S(2)}, u32[]{:S(2)}) async-start(bf16[32,48,128]{2,1,0:T(8,128)(2,1)} %bitcast.2), calls=%async_computation | async-start | bytes 786432 | tf_op jit(solution)/shard_map/all_to_all | solution.py:293
  31.8 0.1 pad_maximum_fusion.w_near
  31.9 0.2 collective-permute-start.4
  32.2 0.0 copy-start
  32.2 0.0 copy-start.3
  32.2 0.0 copy-start.5
  32.2 0.1 pad_maximum_fusion.1.g_near
  32.3 0.0 copy-start.8
  32.3 1.4 %collective-permute-start.8 = (bf16[4,128,512]{2,1,0:T(8,128)(2,1)S(1)}, bf16[4,128,512]{2,1,0:T(8,128)(2,1)S(1)}, u32[]{:S(2)}, u32[]{:S(2)}) collective-permute-start(bf16[4,128,512]{2,1,0:T(8,128)(2,1)S(1)} %pad_maximum_fusion.1.g_near), channel_id=1, source_target_pairs={{0,1},{1,0},{2,3},{3,2},{4,5},{5,4},{6,7},{7,6},{8,9},{9,8},{10,11... | collective-permute-start | bytes 1572872 | tf_op jit(solution)/shard_map/ppermute | solution.py:271
  33.7 0.9 filter_spectrum.1.kernel
  34.6 13.7 %all-to-all-done.streams = bf16[32,48,128]{2,1,0:T(8,128)(2,1)S(1)} async-done(((bf16[32,48,128]{2,1,0:T(8,128)(2,1)}), bf16[32,48,128]{2,1,0:T(8,128)(2,1)S(1)}, u32[]{:S(2)}, u32[]{:S(2)}) %all-to-all-start) | async-done | bytes 393248 | tf_op jit(solution)/shard_map/all_to_all | solution.py:293
  48.4 2.9 %front.1 = (bf16[32,32,512]{2,1,0:T(8,128)(2,1)S(1)}, f32[32,2048]{1,0:T(8,128)S(1)}, f32[32,2048]{1,0:T(8,128)S(1)}, f32[32,2048]{1,0:T(8,128)S(1)}, f32[32,2048]{1,0:T(8,128)S(1)}, /*index=5*/f32[640,256]{1,0:T(8,128)S(1)}) custom-call(bf16[32,48,128]{2,1,0:T(8,128)(2,1)S(1)} %all-to-all-done.streams, f32[3,3,16]{2,1,0:T(4,128)S(1)} %copy-done.9, ...), custom_call_target="tpu_custom_call" | custom-call | tf_op jit(solution)/shard_map/front/pallas_call | solution.py:310
  51.3 1.5 %mixed_grad.1 = bf16[32,32,512]{2,1,0:T(8,128)(2,1)S(1)} custom-call(s32[6]{0:T(128)S(1)} %stack.57.place, bf16[4,512,128]{2,1,0:T(8,128)(2,1)S(1)} %pad_maximum_fusion.w_near, bf16[4,512,128]{2,1,0:T(8,128)(2,1)S(1)} %collective-permute-done.4.w_far, bf16[4,128,512]{2,1,0:T(8,128)(2,1)S(1)} %pad_maximum_fusion.1.g_near, ...), custom_call_target="tpu_custom_call", output_to_operand_aliasing={{}: (5, {})} | custom-call | tf_op jit(solution)/shard_map/mixed_grad/pallas_call | solution.py:325
  52.8 38.3 %all_to_all.15.mixed.upstream = bf16[32,32,512]{2,1,0:T(8,128)(2,1)S(1)} all-to-all(bf16[32,32,512]{2,1,0:T(8,128)(2,1)S(1)} %mixed_grad.1), channel_id=1, replica_groups=mesh['ctx'=32,'tp'=8] {'ctx'}, dimensions={0} | all-to-all | bytes 2097152 | tf_op jit(solution)/shard_map/all_to_all | solution.py:337
  91.1 3.0 %projections.1 = (bf16[4,128,512]{2,1,0:T(8,128)(2,1)S(1)}, bf16[4,128,512]{2,1,0:T(8,128)(2,1)}, bf16[4,512,128]{2,1,0:T(8,128)(2,1)S(1)}, bf16[4,512,128]{2,1,0:T(8,128)(2,1)S(1)}) custom-call(s32[6]{0:T(128)S(1)} %copy-done.12, bf16[32,32,512]{2,1,0:T(8,128)(2,1)S(1)} %all_to_all.15.mixed.upstream, bf16[4,512,128]{2,1,0:T(8,128)(2,1)S(1)} %pad_maximum_fusion.w_near, ...), custom_call_target="tpu_custom_call" | custom-call | tf_op jit(solution)/shard_map/projections/pallas_call | solution.py:339
  94.2 1.5 %collective-permute-start.9 = (bf16[4,128,512]{2,1,0:T(8,128)(2,1)}, bf16[4,128,512]{2,1,0:T(8,128)(2,1)S(1)}, u32[]{:S(2)}, u32[]{:S(2)}) collective-permute-start(bf16[4,128,512]{2,1,0:T(8,128)(2,1)} %get-tuple-element.32), channel_id=1, source_target_pairs={{0,1},{1,0},{2,3},{3,2},{4,5},{5,4},{6,7},{7,6},{8,9},{9,8},{10,11... | collective-permute-start | bytes 1572872 | tf_op jit(solution)/shard_map/ppermute | solution.py:271
  95.7 0.6 copy-done.14
  96.3 4.2 %rear.1 = (bf16[32,48,128]{2,1,0:T(8,128)(2,1)}, f32[16,4096]{1,0:T(8,128)}) custom-call(bf16[32,32,512]{2,1,0:T(8,128)(2,1)S(1)} %all_to_all.15.mixed.upstream, f32[3,3,16]{2,1,0:T(4,128)S(1)} %copy-done.10, f32[16]{0:T(128)S(1)} %copy-done.14, f32[640,256]{1,0:T(8,128)S(1)} %filter_spectrum.1.kernel, f32[640,256]{1,0:T(8,128)S(1)} %get-tuple-element.33.spectrum, ...), custom_call_target="tpu_custom_call" | custom-call | tf_op jit(solution)/shard_map/rear/pallas_call | solution.py:364
  100.6 3.8 %all-to-all-start.2 = ((bf16[32,48,128]{2,1,0:T(8,128)(2,1)}), bf16[32,48,128]{2,1,0:T(8,128)(2,1)S(1)}, u32[]{:S(2)}, u32[]{:S(2)}) async-start(bf16[32,48,128]{2,1,0:T(8,128)(2,1)} %get-tuple-element.38), calls=%async_computation.2 | async-start | bytes 786432 | tf_op jit(solution)/shard_map/all_to_all | solution.py:380
  104.4 0.1 collective-permute-start.14
  104.5 3.5 %collective-permute-done.9 = bf16[4,128,512]{2,1,0:T(8,128)(2,1)S(1)} collective-permute-done((bf16[4,128,512]{2,1,0:T(8,128)(2,1)}, bf16[4,128,512]{2,1,0:T(8,128)(2,1)S(1)}, u32[]{:S(2)}, u32[]{:S(2)}) %collective-permute-start.9) | collective-permute-done | bytes 524320 | tf_op jit(solution)/shard_map/ppermute | solution.py:271
  108.0 0.2 fusion.8
  108.2 0.6 collective-permute-start.10
  108.8 2.3 %collective-permute-start.12 = (bf16[128,512]{1,0:T(8,128)(2,1)S(1)}, bf16[128,512]{1,0:T(8,128)(2,1)S(1)}, u32[]{:S(2)}, u32[]{:S(2)}) collective-permute-start(bf16[128,512]{1,0:T(8,128)(2,1)S(1)} %get-tuple-element.50), channel_id=1, source_target_pairs={{0,6},{1,7},{2,4},{3,5},{4,2},{5,3},{6,0},{7,1},{8,14},{9,15},{10,... | collective-permute-start | bytes 393224 | tf_op jit(solution)/shard_map/ppermute | solution.py:271
  111.1 1.3 collective-permute-start.11
  112.4 0.1 fusion.9
  112.5 0.1 collective-permute-start.15
  112.6 1.5 %collective-permute-start.17 = (bf16[512,128]{1,0:T(8,128)(2,1)S(1)}, bf16[512,128]{1,0:T(8,128)(2,1)S(1)}, u32[]{:S(2)}, u32[]{:S(2)}) collective-permute-start(bf16[512,128]{1,0:T(8,128)(2,1)S(1)} %get-tuple-element.47), channel_id=1, source_target_pairs={{0,144},{8,152},{16,128},{24,136},{32,176},{40,184},{48,160},{56,1... | collective-permute-start | bytes 393224 | tf_op jit(solution)/shard_map/ppermute | solution.py:271
  114.2 3.5 %collective-permute-start.16 = (bf16[512,128]{1,0:T(8,128)(2,1)S(1)}, bf16[512,128]{1,0:T(8,128)(2,1)S(1)}, u32[]{:S(2)}, u32[]{:S(2)}) collective-permute-start(bf16[512,128]{1,0:T(8,128)(2,1)S(1)} %get-tuple-element.48), channel_id=1, source_target_pairs={{0,128},{8,136},{16,144},{24,152},{32,160},{40,168},{48,176},{56,1... | collective-permute-start | bytes 393224 | tf_op jit(solution)/shard_map/ppermute | solution.py:271
  117.6 0.1 fusion.7
  117.7 3.5 %collective-permute-start.13 = (bf16[128,512]{1,0:T(8,128)(2,1)S(1)}, bf16[128,512]{1,0:T(8,128)(2,1)S(1)}, u32[]{:S(2)}, u32[]{:S(2)}) collective-permute-start(bf16[128,512]{1,0:T(8,128)(2,1)S(1)} %fusion.7), channel_id=1, source_target_pairs={{0,0},{1,32},{2,64},{3,96},{4,4},{5,36},{6,68},{7,100},{8,8},{9,40... | collective-permute-start | bytes 393224 | tf_op jit(solution)/shard_map/ppermute | solution.py:281
  121.2 1.2 collective-permute-done.17
  122.4 1.2 collective-permute-done.16
  123.6 0.8 fusion.3
  124.3 0.8 copy.16
  125.1 6.8 %collective-permute-done.13 = bf16[128,512]{1,0:T(8,128)(2,1)S(1)} collective-permute-done((bf16[128,512]{1,0:T(8,128)(2,1)S(1)}, bf16[128,512]{1,0:T(8,128)(2,1)S(1)}, u32[]{:S(2)}, u32[]{:S(2)}) %collective-permute-start.13) | collective-permute-done | bytes 131104 | tf_op jit(solution)/shard_map/ppermute | solution.py:281
  131.9 0.7 copy.19
  (44 shorter events, 0.2 us)
Async XLA Ops:
  0.6 18.3 %collective-permute-start = (bf16[128,512]{1,0:T(8,128)(2,1)}, bf16[128,512]{1,0:T(8,128)(2,1)S(1)}, u32[]{:S(2)}, u32[]{:S(2)}) collective-permute-start(bf16[128,512]{1,0:T(8,128)(2,1)} %param.15), channel_id=1, source_target_pairs={{0,0},{1,32},{2,64},{3,96},{4,4},{5,36},{6,68},{7,100},{8,8},{9,40... | collective-permute-start | bytes 393224 | tf_op jit(solution)/shard_map/ppermute | solution.py:281
  7.8 11.1 %collective-permute-start.2 = (bf16[512,128]{1,0:T(8,128)(2,1)}, bf16[512,128]{1,0:T(8,128)(2,1)S(1)}, u32[]{:S(2)}, u32[]{:S(2)}) collective-permute-start(bf16[512,128]{1,0:T(8,128)(2,1)} %param.14), channel_id=1, source_target_pairs={{0,128},{8,136},{16,144},{24,152},{32,160},{40,168},{48,176},{56,1... | collective-permute-start | bytes 393224 | tf_op jit(solution)/shard_map/ppermute | solution.py:271
  10.5 8.4 %collective-permute-start.1 = (bf16[512,128]{1,0:T(8,128)(2,1)}, bf16[512,128]{1,0:T(8,128)(2,1)S(1)}, u32[]{:S(2)}, u32[]{:S(2)}) collective-permute-start(bf16[512,128]{1,0:T(8,128)(2,1)} %param.14), channel_id=1, source_target_pairs={{0,16},{8,24},{16,0},{24,8},{32,48},{40,56},{48,32},{56,40},{64,80... | collective-permute-start | bytes 393224 | tf_op jit(solution)/shard_map/ppermute | solution.py:271
  11.5 7.8 %collective-permute-start.3 = (bf16[512,128]{1,0:T(8,128)(2,1)}, bf16[512,128]{1,0:T(8,128)(2,1)S(1)}, u32[]{:S(2)}, u32[]{:S(2)}) collective-permute-start(bf16[512,128]{1,0:T(8,128)(2,1)} %param.14), channel_id=1, source_target_pairs={{0,144},{8,152},{16,128},{24,136},{32,176},{40,184},{48,160},{56,1... | collective-permute-start | bytes 393224 | tf_op jit(solution)/shard_map/ppermute | solution.py:271
  14.7 36.6 %copy-start.11 = (s32[6]{0:T(128)}, s32[6]{0:T(128)S(1)}, u32[]{:S(2)}) copy-start(s32[6]{0:T(128)S(1)} %stack.57.place) | copy-start | bytes 76
  19.3 12.5 %copy-start.16 = (bf16[512,128]{1,0:T(8,128)(2,1)S(1)}, bf16[512,128]{1,0:T(8,128)(2,1)}, u32[]{:S(2)}) copy-start(bf16[512,128]{1,0:T(8,128)(2,1)} %param.14) | copy-start | bytes 393220
  19.3 12.8 %collective-permute-start.7 = (bf16[128,512]{1,0:T(8,128)(2,1)S(1)}, bf16[128,512]{1,0:T(8,128)(2,1)S(1)}, u32[]{:S(2)}, u32[]{:S(2)}) collective-permute-start(bf16[128,512]{1,0:T(8,128)(2,1)S(1)} %collective-permute-done), channel_id=1, source_target_pairs={{0,6},{1,7},{2,4},{3,5},{4,2},{5,3},{6,0},{7,1},{8,14},{9,15},{10,... | collective-permute-start | bytes 393224 | tf_op jit(solution)/shard_map/ppermute | solution.py:271
  21.2 10.9 %collective-permute-start.6 = (bf16[128,512]{1,0:T(8,128)(2,1)S(1)}, bf16[128,512]{1,0:T(8,128)(2,1)S(1)}, u32[]{:S(2)}, u32[]{:S(2)}) collective-permute-start(bf16[128,512]{1,0:T(8,128)(2,1)S(1)} %collective-permute-done), channel_id=1, source_target_pairs={{0,4},{1,5},{2,6},{3,7},{4,0},{5,1},{6,2},{7,3},{8,12},{9,13},{10,... | collective-permute-start | bytes 393224 | tf_op jit(solution)/shard_map/ppermute | solution.py:271
  22.3 9.8 %collective-permute-start.5 = (bf16[128,512]{1,0:T(8,128)(2,1)S(1)}, bf16[128,512]{1,0:T(8,128)(2,1)S(1)}, u32[]{:S(2)}, u32[]{:S(2)}) collective-permute-start(bf16[128,512]{1,0:T(8,128)(2,1)S(1)} %collective-permute-done), channel_id=1, source_target_pairs={{0,2},{1,3},{2,0},{3,1},{4,6},{5,7},{6,4},{7,5},{8,10},{9,11},{10,... | collective-permute-start | bytes 393224 | tf_op jit(solution)/shard_map/ppermute | solution.py:271
  23.4 25.0 %all-to-all-start = ((bf16[32,48,128]{2,1,0:T(8,128)(2,1)}), bf16[32,48,128]{2,1,0:T(8,128)(2,1)S(1)}, u32[]{:S(2)}, u32[]{:S(2)}) async-start(bf16[32,48,128]{2,1,0:T(8,128)(2,1)} %bitcast.2), calls=%async_computation | async-start | bytes 786432 | tf_op jit(solution)/shard_map/all_to_all | solution.py:293
  31.9 19.4 %collective-permute-start.4 = (bf16[4,512,128]{2,1,0:T(8,128)(2,1)S(1)}, bf16[4,512,128]{2,1,0:T(8,128)(2,1)S(1)}, u32[]{:S(2)}, u32[]{:S(2)}) collective-permute-start(bf16[4,512,128]{2,1,0:T(8,128)(2,1)S(1)} %pad_maximum_fusion.w_near), channel_id=1, source_target_pairs={{0,8},{8,0},{16,24},{24,16},{32,40},{40,32},{48,56},{56,48},{64,72... | collective-permute-start | bytes 1572872 | tf_op jit(solution)/shard_map/ppermute | solution.py:271
  32.2 1.6 %copy-start = (bf16[2,256,256]{2,1,0:T(8,128)(2,1)S(1)}, bf16[2,256,256]{2,1,0:T(8,128)(2,1)}, u32[]{:S(2)}) copy-start(bf16[2,256,256]{2,1,0:T(8,128)(2,1)} %constant.27.clone.second) | copy-start | bytes 786436
  32.2 1.6 %copy-start.3 = (f32[2,40,128]{2,1,0:T(8,128)S(1)}, f32[2,40,128]{2,1,0:T(8,128)}, u32[]{:S(2)}) copy-start(f32[2,40,128]{2,1,0:T(8,128)} %constant.26.clone.twist) | copy-start | bytes 122884
  32.2 1.5 %copy-start.5 = (bf16[2,80,32]{2,1,0:T(8,128)(2,1)S(1)}, bf16[2,80,32]{2,1,0:T(8,128)(2,1)}, u32[]{:S(2)}) copy-start(bf16[2,80,32]{2,1,0:T(8,128)(2,1)} %constant.25.clone.first) | copy-start | bytes 30724
  32.2 1.5 %copy-start.7 = (f32[16,4096]{1,0:T(8,128)S(1)}, f32[16,4096]{1,0:T(8,128)}, u32[]{:S(2)}) copy-start(f32[16,4096]{1,0:T(8,128)} %filters.1) | copy-start | bytes 786436
  32.3 16.1 %copy-start.8 = (bf16[2,32,80]{2,1,0:T(8,128)(2,1)S(1)}, bf16[2,32,80]{2,1,0:T(8,128)(2,1)}, u32[]{:S(2)}) copy-start(bf16[2,32,80]{2,1,0:T(8,128)(2,1)} %constant.28.clone.last) | copy-start | bytes 30724
  32.3 16.1 %copy-start.9 = (f32[3,3,16]{2,1,0:T(4,128)S(1)}, f32[3,3,16]{2,1,0:T(4,128)}, u32[]{:S(2)}) copy-start(f32[3,3,16]{2,1,0:T(4,128)} %short_w.3) | copy-start | bytes 1732
  32.3 16.1 %copy-start.13 = (f32[16]{0:T(128)S(1)}, f32[16]{0:T(128)}, u32[]{:S(2)}) copy-start(f32[16]{0:T(128)} %skip.3) | copy-start | bytes 196
  32.3 19.0 %collective-permute-start.8 = (bf16[4,128,512]{2,1,0:T(8,128)(2,1)S(1)}, bf16[4,128,512]{2,1,0:T(8,128)(2,1)S(1)}, u32[]{:S(2)}, u32[]{:S(2)}) collective-permute-start(bf16[4,128,512]{2,1,0:T(8,128)(2,1)S(1)} %pad_maximum_fusion.1.g_near), channel_id=1, source_target_pairs={{0,1},{1,0},{2,3},{3,2},{4,5},{5,4},{6,7},{7,6},{8,9},{9,8},{10,11... | collective-permute-start | bytes 1572872 | tf_op jit(solution)/shard_map/ppermute | solution.py:271
  52.8 38.3 %copy-start.12 = (s32[6]{0:T(128)S(1)}, s32[6]{0:T(128)}, u32[]{:S(2)}) copy-start(s32[6]{0:T(128)} %copy-done.11) | copy-start | bytes 76
  91.1 4.6 %copy-start.4 = (f32[2,40,128]{2,1,0:T(8,128)S(1)}, f32[2,40,128]{2,1,0:T(8,128)}, u32[]{:S(2)}) copy-start(f32[2,40,128]{2,1,0:T(8,128)} %constant.26.clone.twist) | copy-start | bytes 122884
  91.1 4.6 %copy-start.6 = (bf16[2,80,32]{2,1,0:T(8,128)(2,1)S(1)}, bf16[2,80,32]{2,1,0:T(8,128)(2,1)}, u32[]{:S(2)}) copy-start(bf16[2,80,32]{2,1,0:T(8,128)(2,1)} %constant.25.clone.first) | copy-start | bytes 30724
  94.2 6.4 %copy-start.1 = (bf16[4,128,512]{2,1,0:T(8,128)(2,1)}, bf16[4,128,512]{2,1,0:T(8,128)(2,1)S(1)}, u32[]{:S(2)}) copy-start(bf16[4,128,512]{2,1,0:T(8,128)(2,1)S(1)} %get-tuple-element.31) | copy-start | bytes 1572868
  94.2 6.4 %copy-start.15 = (bf16[4,512,128]{2,1,0:T(8,128)(2,1)}, bf16[4,512,128]{2,1,0:T(8,128)(2,1)S(1)}, u32[]{:S(2)}) copy-start(bf16[4,512,128]{2,1,0:T(8,128)(2,1)S(1)} %get-tuple-element.41) | copy-start | bytes 1572868
  94.2 1.5 %copy-start.10 = (f32[3,3,16]{2,1,0:T(4,128)S(1)}, f32[3,3,16]{2,1,0:T(4,128)}, u32[]{:S(2)}) copy-start(f32[3,3,16]{2,1,0:T(4,128)} %short_w.3) | copy-start | bytes 1732
  94.2 13.8 %collective-permute-start.9 = (bf16[4,128,512]{2,1,0:T(8,128)(2,1)}, bf16[4,128,512]{2,1,0:T(8,128)(2,1)S(1)}, u32[]{:S(2)}, u32[]{:S(2)}) collective-permute-start(bf16[4,128,512]{2,1,0:T(8,128)(2,1)} %get-tuple-element.32), channel_id=1, source_target_pairs={{0,1},{1,0},{2,3},{3,2},{4,5},{5,4},{6,7},{7,6},{8,9},{9,8},{10,11... | collective-permute-start | bytes 1572872 | tf_op jit(solution)/shard_map/ppermute | solution.py:271
  95.7 0.7 copy-start.14
  100.6 7.4 %copy-start.2 = (bf16[4,128,512]{2,1,0:T(8,128)(2,1)S(1)}, bf16[4,128,512]{2,1,0:T(8,128)(2,1)}, u32[]{:S(2)}) copy-start(bf16[4,128,512]{2,1,0:T(8,128)(2,1)} %copy-done.1) | copy-start | bytes 1572868
  100.6 23.8 %all-to-all-start.2 = ((bf16[32,48,128]{2,1,0:T(8,128)(2,1)}), bf16[32,48,128]{2,1,0:T(8,128)(2,1)S(1)}, u32[]{:S(2)}, u32[]{:S(2)}) async-start(bf16[32,48,128]{2,1,0:T(8,128)(2,1)} %get-tuple-element.38), calls=%async_computation.2 | async-start | bytes 786432 | tf_op jit(solution)/shard_map/all_to_all | solution.py:380
  104.4 8.0 %collective-permute-start.14 = (bf16[4,512,128]{2,1,0:T(8,128)(2,1)}, bf16[4,512,128]{2,1,0:T(8,128)(2,1)S(1)}, u32[]{:S(2)}, u32[]{:S(2)}) collective-permute-start(bf16[4,512,128]{2,1,0:T(8,128)(2,1)} %copy-done.15), channel_id=1, source_target_pairs={{0,8},{8,0},{16,24},{24,16},{32,40},{40,32},{48,56},{56,48},{64,72... | collective-permute-start | bytes 1572872 | tf_op jit(solution)/shard_map/ppermute | solution.py:271
  108.2 6.0 %collective-permute-start.10 = (bf16[128,512]{1,0:T(8,128)(2,1)S(1)}, bf16[128,512]{1,0:T(8,128)(2,1)S(1)}, u32[]{:S(2)}, u32[]{:S(2)}) collective-permute-start(bf16[128,512]{1,0:T(8,128)(2,1)S(1)} %get-tuple-element.49), channel_id=1, source_target_pairs={{0,2},{1,3},{2,0},{3,1},{4,6},{5,7},{6,4},{7,5},{8,10},{9,11},{10,... | collective-permute-start | bytes 393224 | tf_op jit(solution)/shard_map/ppermute | solution.py:271
  108.8 8.8 %collective-permute-start.12 = (bf16[128,512]{1,0:T(8,128)(2,1)S(1)}, bf16[128,512]{1,0:T(8,128)(2,1)S(1)}, u32[]{:S(2)}, u32[]{:S(2)}) collective-permute-start(bf16[128,512]{1,0:T(8,128)(2,1)S(1)} %get-tuple-element.50), channel_id=1, source_target_pairs={{0,6},{1,7},{2,4},{3,5},{4,2},{5,3},{6,0},{7,1},{8,14},{9,15},{10,... | collective-permute-start | bytes 393224 | tf_op jit(solution)/shard_map/ppermute | solution.py:271
  111.1 6.5 %collective-permute-start.11 = (bf16[128,512]{1,0:T(8,128)(2,1)S(1)}, bf16[128,512]{1,0:T(8,128)(2,1)S(1)}, u32[]{:S(2)}, u32[]{:S(2)}) collective-permute-start(bf16[128,512]{1,0:T(8,128)(2,1)S(1)} %get-tuple-element.51), channel_id=1, source_target_pairs={{0,4},{1,5},{2,6},{3,7},{4,0},{5,1},{6,2},{7,3},{8,12},{9,13},{10,... | collective-permute-start | bytes 393224 | tf_op jit(solution)/shard_map/ppermute | solution.py:271
  112.5 8.6 %collective-permute-start.15 = (bf16[512,128]{1,0:T(8,128)(2,1)S(1)}, bf16[512,128]{1,0:T(8,128)(2,1)S(1)}, u32[]{:S(2)}, u32[]{:S(2)}) collective-permute-start(bf16[512,128]{1,0:T(8,128)(2,1)S(1)} %get-tuple-element.46), channel_id=1, source_target_pairs={{0,16},{8,24},{16,0},{24,8},{32,48},{40,56},{48,32},{56,40},{64,80... | collective-permute-start | bytes 393224 | tf_op jit(solution)/shard_map/ppermute | solution.py:271
  112.6 9.8 %collective-permute-start.17 = (bf16[512,128]{1,0:T(8,128)(2,1)S(1)}, bf16[512,128]{1,0:T(8,128)(2,1)S(1)}, u32[]{:S(2)}, u32[]{:S(2)}) collective-permute-start(bf16[512,128]{1,0:T(8,128)(2,1)S(1)} %get-tuple-element.47), channel_id=1, source_target_pairs={{0,144},{8,152},{16,128},{24,136},{32,176},{40,184},{48,160},{56,1... | collective-permute-start | bytes 393224 | tf_op jit(solution)/shard_map/ppermute | solution.py:271
  114.2 9.4 %collective-permute-start.16 = (bf16[512,128]{1,0:T(8,128)(2,1)S(1)}, bf16[512,128]{1,0:T(8,128)(2,1)S(1)}, u32[]{:S(2)}, u32[]{:S(2)}) collective-permute-start(bf16[512,128]{1,0:T(8,128)(2,1)S(1)} %get-tuple-element.48), channel_id=1, source_target_pairs={{0,128},{8,136},{16,144},{24,152},{32,160},{40,168},{48,176},{56,1... | collective-permute-start | bytes 393224 | tf_op jit(solution)/shard_map/ppermute | solution.py:271
  117.7 14.2 %collective-permute-start.13 = (bf16[128,512]{1,0:T(8,128)(2,1)S(1)}, bf16[128,512]{1,0:T(8,128)(2,1)S(1)}, u32[]{:S(2)}, u32[]{:S(2)}) collective-permute-start(bf16[128,512]{1,0:T(8,128)(2,1)S(1)} %fusion.7), channel_id=1, source_target_pairs={{0,0},{1,32},{2,64},{3,96},{4,4},{5,36},{6,68},{7,100},{8,8},{9,40... | collective-permute-start | bytes 393224 | tf_op jit(solution)/shard_map/ppermute | solution.py:281
